TPU v7x, 32 devices: a whole 2x2x4 slice. The times are simulated.
32 devices in a mesh: page: 16 (over z, y, core), strip: 2 (over x).
Axes of the slice: x: 2, y: 2, z: 4, core: 2. Of those that a mesh axis runs over, the one named last changes fastest.
Arguments:
- features: bfloat16 [16, 32, 32, 512], P('page', 'strip'), may hold values from -6 to 6
- quarter_turns: int32 [16], P('page'), may hold values from 0 to 3, as said below
- heights: int32 [16], P('page'), may hold values from 8 to 32, as said below
- widths: int32 [16], P('page'), may hold values from 8 to 32, as said below
- frozen_scale: float32 [2, 512], replicated, may hold values from 0.5 to 2
- frozen_shift: float32 [2, 512], replicated, may hold values from -3 to 3
- first_kernel: bfloat16 [3, 3, 512, 512], replicated, may hold values from -0.09375 to 0.09375
- second_kernel: bfloat16 [3, 3, 512, 512], replicated, may hold values from -0.09375 to 0.09375
- project_weight: bfloat16 [512, 256], replicated, may hold values from -0.25 to 0.25
- project_bias: float32 [256], replicated, may hold values from -3 to 3
- query_weight: bfloat16 [256, 256], replicated, may hold values from -0.375 to 0.375
- query_bias: float32 [256], replicated, may hold values from -3 to 3
- key_weight: bfloat16 [256, 256], replicated, may hold values from -0.375 to 0.375
- value_weight: bfloat16 [256, 256], replicated, may hold values from -0.375 to 0.375
- value_bias: float32 [256], replicated, may hold values from -3 to 3
- output_weight: bfloat16 [256, 256], replicated, may hold values from -1.5 to 1.5
- output_bias: float32 [256], replicated, may hold values from -3 to 3
- first_gain: float32 [256], replicated, may hold values from 0.1 to 1.9
- first_shift: float32 [256], replicated, may hold values from -3 to 3
- expand_weight: bfloat16 [256, 2048], replicated, may hold values from -0.375 to 0.375
- expand_bias: float32 [2048], replicated, may hold values from -3 to 3
- shrink_weight: bfloat16 [2048, 256], replicated, may hold values from -0.125 to 0.125
- shrink_bias: float32 [256], replicated, may hold values from -3 to 3
- final_gain: float32 [256], replicated, may hold values from 0.1 to 1.9
- final_shift: float32 [256], replicated, may hold values from -3 to 3
- cotangent: bfloat16 [16, 32, 32, 256], P('page', 'strip'), may hold values from -6 to 6
Outputs:
- encoded: bfloat16 [16, 32, 32, 256], P('page', 'strip')
- features_grad: float32 [16, 32, 32, 512], P('page', 'strip')
- first_kernel_grad: float32 [3, 3, 512, 512], P(None, None, 'page', 'strip')
- second_kernel_grad: float32 [3, 3, 512, 512], P(None, None, 'page', 'strip')
- project_weight_grad: float32 [512, 256], replicated
- project_bias_grad: float32 [256], replicated
- query_weight_grad: float32 [256, 256], replicated
- query_bias_grad: float32 [256], replicated
- key_weight_grad: float32 [256, 256], replicated
- value_weight_grad: float32 [256, 256], replicated
- value_bias_grad: float32 [256], replicated
- output_weight_grad: float32 [256, 256], replicated
- output_bias_grad: float32 [256], replicated
- first_gain_grad: float32 [256], replicated
- first_shift_grad: float32 [256], replicated
- expand_weight_grad: float32 [256, 2048], replicated
- expand_bias_grad: float32 [2048], replicated
- shrink_weight_grad: float32 [2048, 256], replicated
- shrink_bias_grad: float32 [256], replicated
- final_gain_grad: float32 [256], replicated
- final_shift_grad: float32 [256], replicated
Inputs may be any that keep to these rules, and one draw needn't show every extreme that they name: `quarter_turns`: in every block of 1 consecutive pages one page, drawn from the seed, has valid cells in every stored row: its height is 32 and its quarter turns are 0 or 2, or its width is 32 and its quarter turns are 1 or 3. `heights`: drawn together with quarter_turns and widths as stated there. `widths`: drawn together with quarter_turns and heights as stated there.
All inputs are finite; a program needn't handle non-finite values.
Results may differ from a plain program's by a relative error of at most 0.035.
Values may be sent and summed in bfloat16 or wider, within the bound.
A program may use at most 128 MiB of HBM per device.

v0:
```python
import math

import jax
import jax.numpy as jnp
from jax import lax
from jax.sharding import PartitionSpec as P

HEADS = 8


def with_halo(block, sides, width):
    for axis, dim in sides:
        count = lax.axis_size(axis)
        forward = [(i, i + 1) for i in range(count - 1)]
        backward = [(target, source) for source, target in forward]
        low = lax.ppermute(
            lax.slice_in_dim(block, block.shape[dim] - width, None, axis=dim), axis, forward
        )
        high = lax.ppermute(lax.slice_in_dim(block, 0, width, axis=dim), axis, backward)
        block = jnp.concatenate([low, block, high], axis=dim)
    return block


def gelu_exact(value):
    return jax.nn.gelu(value, approximate=False)


def gelu_back(value, upstream):
    return jax.vjp(gelu_exact, value)[1](upstream)[0]


def layer_norm(value, gain, shift):
    center = value - jnp.mean(value, axis=-1, keepdims=True)
    spread = jnp.mean(center * center, axis=-1, keepdims=True)
    return center * lax.rsqrt(spread + 1e-05) * gain + shift


def sine_positions(turns, heights, widths, row_start, rows, side, width):
    row = row_start + jnp.arange(rows, dtype=jnp.int32)[None, :, None]
    column = jnp.arange(side, dtype=jnp.int32)[None, None, :]
    turn = turns[:, None, None]
    upright_y = jnp.where(
        turn == 0,
        row,
        jnp.where(turn == 1, column, jnp.where(turn == 2, side - 1 - row, side - 1 - column)),
    )
    upright_x = jnp.where(
        turn == 0,
        column,
        jnp.where(turn == 1, side - 1 - row, jnp.where(turn == 2, side - 1 - column, row)),
    )
    valid = (upright_y < heights[:, None, None]) & (upright_x < widths[:, None, None])
    half = width // 2
    index = jnp.arange(half, dtype=jnp.int32)
    period = 10000.0 ** (2.0 * (index // 2).astype(jnp.float32) / half)
    even = index % 2 == 0
    along_y = (
        (upright_y + 1).astype(jnp.float32)
        / (heights[:, None, None].astype(jnp.float32) + 1e-06)
        * (2.0 * math.pi)
    )
    along_x = (
        (upright_x + 1).astype(jnp.float32)
        / (widths[:, None, None].astype(jnp.float32) + 1e-06)
        * (2.0 * math.pi)
    )
    phase_y = along_y[..., None] / period
    phase_x = along_x[..., None] / period
    pos_y = jnp.where(even, jnp.sin(phase_y), jnp.cos(phase_y))
    pos_x = jnp.where(even, jnp.sin(phase_x), jnp.cos(phase_x))
    return (jnp.concatenate([pos_y, pos_x], axis=-1), valid)


def pad_columns(value):
    return jnp.pad(value, ((0, 0), (0, 0), (1, 1), (0, 0)))


def conv_valid(padded, kernel):
    return lax.conv_general_dilated(
        padded,
        kernel,
        (1, 1),
        "VALID",
        dimension_numbers=("NHWC", "HWIO", "NHWC"),
        preferred_element_type=jnp.float32,
    )


def flipped(kernel):
    return jnp.transpose(kernel[::-1, ::-1], (0, 1, 3, 2))


def kernel_grad(padded, upstream):
    rows, side, channels = (upstream.shape[1], upstream.shape[2], upstream.shape[3])
    terms = []
    for down in range(3):
        for across in range(3):
            window = padded[:, down : down + rows, across : across + side, :]
            terms.append(
                jnp.einsum("prci,prco->io", window, upstream, preferred_element_type=jnp.float32)
            )
    return jnp.stack(terms).reshape(3, 3, padded.shape[3], channels)


def left_product(left, right):
    return jnp.einsum("ti,to->io", left, right, preferred_element_type=jnp.float32)


def right_back(upstream, weight):
    return jnp.einsum("to,io->ti", upstream, weight, preferred_element_type=jnp.float32)


def column_sum(value):
    return jnp.sum(value.astype(jnp.float32), axis=0)


def body(
    features,
    quarter_turns,
    heights,
    widths,
    frozen_scale,
    frozen_shift,
    first_kernel,
    second_kernel,
    project_weight,
    project_bias,
    query_weight,
    query_bias,
    key_weight,
    value_weight,
    value_bias,
    output_weight,
    output_bias,
    first_gain,
    first_shift,
    expand_weight,
    expand_bias,
    shrink_weight,
    shrink_bias,
    final_gain,
    final_shift,
    cotangent,
):
    pages, rows, side, channels = features.shape
    width = project_weight.shape[1]
    head_size = width // HEADS
    length = rows * side
    strips = lax.axis_size("strip")
    whole = strips * length
    row_start = lax.axis_index("strip") * rows
    factor = head_size ** (-0.5)
    padded_in = pad_columns(with_halo(features, (("strip", 1),), 1))
    first_pre = conv_valid(padded_in, first_kernel) * frozen_scale[0] + frozen_shift[0]
    hidden = gelu_exact(first_pre).astype(jnp.bfloat16)
    padded_hidden = pad_columns(with_halo(hidden, (("strip", 1),), 1))
    second_pre = (
        conv_valid(padded_hidden, second_kernel) * frozen_scale[1]
        + frozen_shift[1]
        + features.astype(jnp.float32)
    )
    block = gelu_exact(second_pre).astype(jnp.bfloat16).reshape(pages * length, channels)
    source = jnp.dot(block, project_weight, preferred_element_type=jnp.float32) + project_bias
    position, valid = sine_positions(quarter_turns, heights, widths, row_start, rows, side, width)
    joint = (source + position.reshape(pages * length, width)).astype(jnp.bfloat16)
    plain = source.astype(jnp.bfloat16)
    queries = (
        jnp.dot(joint, query_weight, preferred_element_type=jnp.float32) + query_bias
    ).astype(jnp.bfloat16)
    queries = queries.reshape(pages, length, HEADS, head_size)
    keys_local = (
        jnp.dot(joint, key_weight, preferred_element_type=jnp.float32)
        .astype(jnp.bfloat16)
        .reshape(pages, length, width)
    )
    values_local = (
        (jnp.dot(plain, value_weight, preferred_element_type=jnp.float32) + value_bias)
        .astype(jnp.bfloat16)
        .reshape(pages, length, width)
    )
    key_bias = jnp.where(valid, 0.0, -10000.0).astype(jnp.bfloat16).reshape(pages, length)
    keys_piece = lax.all_gather(keys_local, "strip", axis=1, tiled=True)
    values_piece = lax.all_gather(values_local, "strip", axis=1, tiled=True)
    bias_piece = lax.all_gather(key_bias, "strip", axis=1, tiled=True)
    count = keys_piece.shape[1]
    partial_scores = jnp.einsum(
        "pqhd,pkhd->phqk",
        queries,
        keys_piece.reshape(pages, count, HEADS, head_size),
        preferred_element_type=jnp.float32,
    )
    partial_scores = partial_scores * factor + bias_piece.astype(jnp.float32)[:, None, None, :]
    peak = jnp.max(partial_scores, axis=-1)
    expd = jnp.exp(partial_scores - peak[..., None])
    denom = jnp.sum(expd, axis=-1)
    logsum = peak + jnp.log(denom)
    low_prob = (expd / denom[..., None]).astype(jnp.bfloat16)
    mixed = jnp.einsum(
        "phqk,pkhd->pqhd",
        low_prob,
        values_piece.reshape(pages, whole, HEADS, head_size),
        preferred_element_type=jnp.float32,
    )
    combined = mixed.reshape(pages * length, width).astype(jnp.bfloat16)
    attended = jnp.dot(combined, output_weight, preferred_element_type=jnp.float32) + output_bias
    first_sum = source + attended
    normed = layer_norm(first_sum, first_gain, first_shift)
    ff_in = normed.astype(jnp.bfloat16)
    expanded = jnp.dot(ff_in, expand_weight, preferred_element_type=jnp.float32) + expand_bias
    activated = gelu_exact(expanded).astype(jnp.bfloat16)
    second_sum = (
        normed + jnp.dot(activated, shrink_weight, preferred_element_type=jnp.float32) + shrink_bias
    )
    result, final_back = jax.vjp(layer_norm, second_sum, final_gain, final_shift)
    encoded = result.astype(jnp.bfloat16).reshape(pages, rows, side, width)
    d_second, final_gain_grad, final_shift_grad = final_back(
        cotangent.astype(jnp.float32).reshape(pages * length, width)
    )
    d_shrunk = d_second.astype(jnp.bfloat16)
    shrink_bias_grad = column_sum(d_shrunk)
    shrink_weight_grad = left_product(activated, d_shrunk)
    d_expanded = gelu_back(expanded, right_back(d_shrunk, shrink_weight)).astype(jnp.bfloat16)
    expand_bias_grad = column_sum(d_expanded)
    expand_weight_grad = left_product(ff_in, d_expanded)
    d_normed = right_back(d_expanded, expand_weight) + d_second
    d_first, first_gain_grad, first_shift_grad = jax.vjp(
        layer_norm, first_sum, first_gain, first_shift
    )[1](d_normed)
    d_attended = d_first.astype(jnp.bfloat16)
    output_bias_grad = column_sum(d_attended)
    output_weight_grad = left_product(combined, d_attended)
    d_combined = (
        right_back(d_attended, output_weight)
        .astype(jnp.bfloat16)
        .reshape(pages, length, HEADS, head_size)
    )
    delta = jnp.sum(d_combined.astype(jnp.float32) * mixed, axis=-1)
    logsum_rows = jnp.transpose(logsum, (0, 2, 1))
    keys_all, values_again, bias_all = (
        lax.all_gather(keys_local, "strip", axis=1, tiled=True),
        lax.all_gather(values_local, "strip", axis=1, tiled=True),
        lax.all_gather(key_bias, "strip", axis=1, tiled=True),
    )
    keys_four = keys_all.reshape(pages, whole, HEADS, head_size)
    values_four = values_again.reshape(pages, whole, HEADS, head_size)
    part_scores = (
        jnp.einsum("pqhd,pkhd->phqk", queries, keys_four, preferred_element_type=jnp.float32)
        * factor
    )
    part_scores = part_scores + bias_all.astype(jnp.float32)[:, None, None, :]
    prob = jnp.exp(part_scores - jnp.transpose(logsum_rows, (0, 2, 1))[..., None])
    d_prob = jnp.einsum(
        "pqhd,pkhd->phqk", d_combined, values_four, preferred_element_type=jnp.float32
    )
    pair_d_scores = (prob * (d_prob - jnp.transpose(delta, (0, 2, 1))[..., None])).astype(
        jnp.bfloat16
    )
    weights_low = prob.astype(jnp.bfloat16)
    d_queries = factor * jnp.einsum(
        "phqk,pkhd->pqhd", pair_d_scores, keys_four, preferred_element_type=jnp.float32
    )
    key_part = factor * jnp.einsum(
        "phqk,pqhd->kphd", pair_d_scores, queries, preferred_element_type=jnp.float32
    )
    value_part = jnp.einsum(
        "phqk,pqhd->kphd", weights_low, d_combined, preferred_element_type=jnp.float32
    )
    summed = lax.psum_scatter(
        jnp.concatenate(
            [
                key_part.reshape(length * lax.axis_size("strip"), pages, width),
                value_part.reshape(length * lax.axis_size("strip"), pages, width),
            ],
            axis=-1,
        ).astype(jnp.bfloat16),
        "strip",
        scatter_dimension=0,
        tiled=True,
    ).astype(jnp.float32)
    d_keys = jnp.transpose(summed[:, :, :width], (1, 0, 2))
    d_values = jnp.transpose(summed[:, :, width:], (1, 0, 2))
    d_queries_low = d_queries.reshape(pages * length, width).astype(jnp.bfloat16)
    d_keys_low = d_keys.reshape(pages * length, width).astype(jnp.bfloat16)
    d_values_low = d_values.reshape(pages * length, width).astype(jnp.bfloat16)
    query_bias_grad = column_sum(d_queries_low)
    query_weight_grad = left_product(joint, d_queries_low)
    key_weight_grad = left_product(joint, d_keys_low)
    value_weight_grad = left_product(plain, d_values_low)
    value_bias_grad = column_sum(d_values_low)
    d_source = (
        d_first
        + right_back(d_queries_low, query_weight)
        + right_back(d_keys_low, key_weight)
        + right_back(d_values_low, value_weight)
    )
    d_source_low = d_source.astype(jnp.bfloat16)
    project_bias_grad = column_sum(d_source_low)
    project_weight_grad = left_product(block, d_source_low)
    d_block = right_back(d_source_low, project_weight).reshape(pages, rows, side, channels)
    d_second_pre = gelu_back(second_pre, d_block)
    d_late = (d_second_pre * frozen_scale[1]).astype(jnp.bfloat16)
    padded_late = pad_columns(with_halo(d_late, (("strip", 1),), 1))
    d_hidden = conv_valid(padded_late, flipped(second_kernel))
    second_kernel_grad = kernel_grad(padded_hidden, d_late)
    d_early = (gelu_back(first_pre, d_hidden) * frozen_scale[0]).astype(jnp.bfloat16)
    padded_early = pad_columns(with_halo(d_early, (("strip", 1),), 1))
    features_grad = conv_valid(padded_early, flipped(first_kernel)) + d_second_pre
    first_kernel_grad = kernel_grad(padded_in, d_early)
    first_part, second_part = (
        lax.psum_scatter(
            first_kernel_grad.astype(jnp.bfloat16), "page", scatter_dimension=2, tiled=True
        ).astype(jnp.float32),
        lax.psum_scatter(
            second_kernel_grad.astype(jnp.bfloat16), "page", scatter_dimension=2, tiled=True
        ).astype(jnp.float32),
    )
    first_part, second_part = (
        lax.psum_scatter(
            first_part.astype(jnp.bfloat16), "strip", scatter_dimension=3, tiled=True
        ).astype(jnp.float32),
        lax.psum_scatter(
            second_part.astype(jnp.bfloat16), "strip", scatter_dimension=3, tiled=True
        ).astype(jnp.float32),
    )
    dense = lax.psum(
        (
            project_weight_grad,
            project_bias_grad,
            query_weight_grad,
            query_bias_grad,
            key_weight_grad,
            value_weight_grad,
            value_bias_grad,
            output_weight_grad,
            output_bias_grad,
            first_gain_grad,
            first_shift_grad,
            expand_weight_grad,
            expand_bias_grad,
            shrink_weight_grad,
            shrink_bias_grad,
            final_gain_grad,
            final_shift_grad,
        ),
        ("page", "strip"),
    )
    return (encoded, features_grad, first_part, second_part) + tuple(dense)


def solution(mesh):
    return jax.shard_map(
        body,
        mesh=mesh,
        in_specs=(
            P("page", "strip", None, None),
            P("page"),
            P("page"),
            P("page"),
            P(),
            P(),
            P(),
            P(),
            P(),
            P(),
            P(),
            P(),
            P(),
            P(),
            P(),
            P(),
            P(),
            P(),
            P(),
            P(),
            P(),
            P(),
            P(),
            P(),
            P(),
            P("page", "strip", None, None),
        ),
        out_specs=(
            P("page", "strip", None, None),
            P("page", "strip", None, None),
            P(None, None, "page", "strip"),
            P(None, None, "page", "strip"),
            P(),
            P(),
            P(),
            P(),
            P(),
            P(),
            P(),
            P(),
            P(),
            P(),
            P(),
            P(),
            P(),
            P(),
            P(),
            P(),
            P(),
        ),
        check_vma=False,
    )
```

profile of v0, /device:TPU:0, one launch (start us, length us, event | category | flops | bytes accessed | tf_op | source)
XLA Modules:
  0.0 531.0 jit_solution(15498364616639855454)
XLA Ops:
  9.4 4.8 collective-permute-start
  17.5 1.9 cosine_select_fusion.1
  25.0 7.0 %multiply_convert_fusion.3 = (bf16[16,8,5,512]{3,1,2,0:T(8,128)(2,1)S(1)}, f32[16,8,5,512]{3,1,2,0:T(8,128)}) fusion(f32[512]{0:T(512)S(1)} %bitcast.520, f32[512]{0:T(512)S(1)} %bitcast.517, bf16[3,3,512,512]{3,2,1,0:T(8,128)(2,1)S(1)} %copy-done.83, bf16[18,1,7,2,512]{4,2,3,0,1:T(8,128)(2,1)S(1)} %slice.152, bf16[18,1,8,5,512]{4,2,3,0,1:T(8,128)(2,1)S(1)} %copy.91, ...), kind=kOutput, calls=%fused_computation.64 | convolution fusion | flops 3045277696 | bytes 7684136 | tf_op jit(solution)/shard_map/conv_general_dilated | solution.py:79
  34.7 5.1 all_gather.14
  42.6 5.3 fusion.17
  48.9 3.6 multiply_convert_fusion.5
  54.2 7.3 %all-gather = bf16[1024,256]{1,0:T(8,128)(2,1)S(1)} all-gather(bf16[512,256]{1,0:T(8,128)(2,1)S(1)} %fusion.87), channel_id=2, replica_groups=mesh['page'=16,'strip'=2] {'strip'}, dimensions={0}, use_global_device_ids=true | all-gather | bytes 786432 | tf_op jit(solution)/shard_map/all_gather | solution.py:183
  63.6 7.0 %all-gather.1 = bf16[1024,256]{1,0:T(8,128)(2,1)S(1)} all-gather(bf16[512,256]{1,0:T(8,128)(2,1)S(1)} %convolution_convert_fusion.1), channel_id=3, replica_groups=mesh['page'=16,'strip'=2] {'strip'}, dimensions={0}, use_global_device_ids=true | all-gather | bytes 786432 | tf_op jit(solution)/shard_map/all_gather | solution.py:182
  72.9 3.7 fusion.253
  76.7 3.7 fusion
  80.5 4.8 fusion.254
  86.1 9.4 %multiply_convert_fusion.1 = (bf16[512,2048]{1,0:T(8,128)(2,1)S(1)}, f32[512,2048]{1,0:T(8,128)S(1)}, f32[512,2048]{1,0:T(8,128)S(1)}) fusion(f32[2048]{0:T(1024)S(1)} %copy-done.85, bf16[256,2048]{1,0:T(8,128)(2,1)S(1)} %copy-done, f32[512,256]{1,0:T(8,128)S(1)} %get-tuple-element.127, f32[256]{0:T(256)S(1)} %copy-done.69, f32[256]{0:T(256)S(1)} %copy-done.63, ...), kind=kOutput, calls=%fused_computation.14 | convolution fusion | flops 606732288 | bytes 12072960 | tf_op jit(solution)/shard_map/dot_general | solution.py:209
  99.6 3.4 convert_reduce_fusion
  106.5 3.6 fusion.44
  110.1 7.7 %multiply_convert_fusion = bf16[8,512,1024]{2,1,0:T(8,128)(2,1)} fusion(f32[8,512,1024]{2,1,0:T(8,128)S(1)} %get-tuple-element.123, bf16[512,8,32]{0,2,1:T(8,128)(2,1)S(1)} %bitcast.480, bf16[1024,8,32]{0,2,1:T(8,128)(2,1)} %bitcast.505, f32[8,512]{1,0:T(8,128)} %bitcast.513, f32[8,512]{1,0:T(8,128)S(1)} %log_add_fusion), kind=kOutput, calls=%fused_computation | convolution fusion | flops 285212672 | bytes 25985024 | tf_op jit(solution)/shard_map/pqhd,pkhd->phqk/dot_general | solution.py:252
  117.8 5.0 fusion.25
  124.2 6.1 %convert_reduce_fusion.5 = (f32[8,32]{1,0:T(8,128)S(1)}, bf16[8,32,512]{2,1,0:T(8,128)(2,1)S(1)}) fusion(bf16[1024,8,32]{0,2,1:T(8,128)(2,1)S(1)} %bitcast.474, bf16[8,512,1024]{2,1,0:T(8,128)(2,1)} %multiply_convert_fusion), kind=kOutput, calls=%fused_computation.261 | convolution fusion | flops 268959488 | bytes 9176064 | tf_op jit(solution)/shard_map/phqk,pkhd->pqhd/dot_general | solution.py:259
  131.3 15.7 %reduce-scatter.6.cloned.1.call-done = bf16[512,1,512]{0,2,1:T(8,128)(2,1)} async-done(((bf16[1024,1,512]{0,2,1:T(8,128)(2,1)}), bf16[512,1,512]{0,2,1:T(8,128)(2,1)}) %reduce-scatter.6.cloned.1.call-update) | async-done | bytes 524304 | tf_op jit(solution)/shard_map/reduce_scatter | solution.py:268
  150.5 2.2 multiply_convert_fusion.4
  167.2 2.2 collective-permute-start.4
  171.3 4.3 collective-permute-done.5
  177.5 8.7 %multiply_convert_fusion.2 = bf16[16,8,5,512]{3,1,2,0:T(8,128)(2,1)S(1)} fusion(bf16[3,3,512,512]{3,2,1,0:T(8,128)(2,1)} %param.33, f32[16,8,5,512]{3,1,2,0:T(8,128)S(1)} %copy-done.89, bf16[18,1,7,2,512]{4,2,3,0,1:T(8,128)(2,1)S(1)} %slice.164, bf16[18,1,8,5,512]{4,2,3,0,1:T(8,128)(2,1)S(1)} %copy.107, f32[512]{0:T(512)S(1)} %bitcast.518, ...), kind=kOutput, calls=%fused_computation.63 | convolution fusion | flops 3047243776 | bytes 7682088 | tf_op jit(solution)/shard_map/conv_general_dilated | solution.py:79
  202.4 2.1 fusion.261
  204.4 37.4 %reduce-scatter.12.cloned.1.call-done = bf16[3,3,32,512]{3,2,1,0:T(8,128)(2,1)} async-done(((bf16[3,3,512,512]{3,2,1,0:T(8,128)(2,1)}), bf16[3,3,32,512]{3,2,1,0:T(8,128)(2,1)}) %reduce-scatter.12.cloned.1.call-update) | async-done | bytes 294928 | tf_op jit(solution)/shard_map/reduce_scatter | solution.py:313
  241.9 1.9 fusion.260
  244.8 3.9 fusion.238
  248.6 71.7 %reduce-scatter.8.cloned.1.call-done = bf16[3,3,32,512]{3,2,1,0:T(8,128)(2,1)} async-done(((bf16[3,3,512,512]{3,2,1,0:T(8,128)(2,1)}), bf16[3,3,32,512]{3,2,1,0:T(8,128)(2,1)}) %reduce-scatter.8.cloned.1.call-update) | async-done | bytes 294928 | tf_op jit(solution)/shard_map/reduce_scatter | solution.py:310
  325.5 3.4 collective-permute-start.6
  330.4 41.2 %all-reduce.2 = (f32[256]{0:T(256)}, f32[256]{0:T(256)}, f32[256]{0:T(256)}, f32[256]{0:T(256)}, f32[256]{0:T(256)}, /*index=5*/f32[256]{0:T(256)}, f32[2048]{0:...) all-reduce(f32[256]{0:T(256)S(1)} %get-tuple-element.132, ...), channel_id=1, replica_groups=mesh['page'=16,'strip'=2] {'page','strip'}, use_global_device_ids=true, to_apply=%region_18.19 | all-reduce | flops 4352 | bytes 34816 | tf_op jit(solution)/shard_map/psum | solution.py:325
  373.9 3.2 convolution_select_fusion
  383.5 128.8 %all-reduce.6.cloned.1.call-done = (f32[512,256]{1,0:T(8,128)}, f32[256,256]{1,0:T(8,128)}, f32[256,256]{1,0:T(8,128)}, f32[256,256]{1,0:T(8,128)}, f32[256,256]...) async-done(((f32[512,256]{1,0:T(8,128)}, f32[256,256]{1,0:T(8,128)}, f32[256,256]{1,0:T(8,128)}, f32[256,256]{1,0:T(8,128)}, f32[256,256]{1,0:T(8,128)}, ...) | async-done | bytes 5767184 | tf_op jit(solution)/shard_map/psum | solution.py:325
  512.3 2.0 copy.235
  (348 shorter events, 95.0 us)
Async XLA Ops:
  7.2 78.9 %copy-start = (bf16[256,2048]{1,0:T(8,128)(2,1)S(1)}, bf16[256,2048]{1,0:T(8,128)(2,1)}, u32[]{:S(2)}) copy-start(bf16[256,2048]{1,0:T(8,128)(2,1)} %param.45) | copy-start | bytes 3145732
  7.2 139.8 %reduce-scatter.6.cloned.1.call-start = ((), (), s32[]{:S(2)}) async-start(), calls=%async_computation.5 | async-start | bytes 1572864 | tf_op jit(solution)/shard_map/reduce_scatter | solution.py:268
  8.1 13.7 %collective-permute-start.1 = (bf16[1,1,32,512]{3,2,1,0:T(8,128)(2,1)S(1)}, bf16[1,1,32,512]{3,2,1,0:T(8,128)(2,1)S(1)}, u32[]{:S(2)}, u32[]{:S(2)}) collective-permute-start(bf16[1,1,32,512]{3,2,1,0:T(8,128)(2,1)S(1)} %get-tuple-element.108), channel_id=1, source_target_pairs={{1,0},{3,2},{5,4},{7,6},{9,8},{11,10},{13,12},{15,14},{17,16},{19,... | collective-permute-start | bytes 98312 | tf_op jit(solution)/shard_map/ppermute | solution.py:19
  9.4 11.3 %collective-permute-start = (bf16[1,1,32,512]{3,2,1,0:T(8,128)(2,1)S(1)}, bf16[1,1,32,512]{3,2,1,0:T(8,128)(2,1)S(1)}, u32[]{:S(2)}, u32[]{:S(2)}) collective-permute-start(bf16[1,1,32,512]{3,2,1,0:T(8,128)(2,1)S(1)} %get-tuple-element.109), channel_id=1, source_target_pairs={{0,1},{2,3},{4,5},{6,7},{8,9},{10,11},{12,13},{14,15},{16,17},{18,... | collective-permute-start | bytes 98312 | tf_op jit(solution)/shard_map/ppermute | solution.py:16
  17.0 25.5 %copy-start.65 = (f32[1,512]{1,0:T(1,128)}, f32[1,512]{1,0:T(1,128)S(1)}, u32[]{:S(2)}) copy-start(f32[1,512]{1,0:T(1,128)S(1)} %get-tuple-element.112) | copy-start | bytes 6148
  32.0 8.4 %collective-permute-start.2 = (bf16[1,1,32,512]{3,2,1,0:T(8,128)(2,1)S(1)}, bf16[1,1,32,512]{3,2,1,0:T(8,128)(2,1)S(1)}, u32[]{:S(2)}, u32[]{:S(2)}) collective-permute-start(bf16[1,1,32,512]{3,2,1,0:T(8,128)(2,1)S(1)} %slice.154), channel_id=1, source_target_pairs={{0,1},{2,3},{4,5},{6,7},{8,9},{10,11},{12,13},{14,15},{16,17},{18,... | collective-permute-start | bytes 98312 | tf_op jit(solution)/shard_map/ppermute | solution.py:16
  33.4 7.0 %collective-permute-start.3 = (bf16[1,1,32,512]{3,2,1,0:T(8,128)(2,1)S(1)}, bf16[1,1,32,512]{3,2,1,0:T(8,128)(2,1)S(1)}, u32[]{:S(2)}, u32[]{:S(2)}) collective-permute-start(bf16[1,1,32,512]{3,2,1,0:T(8,128)(2,1)S(1)} %slice.157), channel_id=1, source_target_pairs={{1,0},{3,2},{5,4},{7,6},{9,8},{11,10},{13,12},{15,14},{17,16},{19,... | collective-permute-start | bytes 98312 | tf_op jit(solution)/shard_map/ppermute | solution.py:19
  85.8 18.6 %copy-start.5 = (f32[512,256]{1,0:T(8,128)}, f32[512,256]{1,0:T(8,128)S(1)}, u32[]{:S(2)}) copy-start(f32[512,256]{1,0:T(8,128)S(1)} %get-tuple-element.127) | copy-start | bytes 1572868
  123.9 117.9 %reduce-scatter.12.cloned.1.call-start = ((), (), s32[]{:S(2)}) async-start(), calls=%async_computation.8 | async-start | bytes 5013504 | tf_op jit(solution)/shard_map/reduce_scatter | solution.py:313
  130.2 19.9 %copy-start.23 = (bf16[8,32,512]{2,1,0:T(8,128)(2,1)}, bf16[8,32,512]{2,1,0:T(8,128)(2,1)S(1)}, u32[]{:S(2)}) copy-start(bf16[8,32,512]{2,1,0:T(8,128)(2,1)S(1)} %get-tuple-element.135) | copy-start | bytes 786436
  131.3 19.2 %copy-start.10 = (bf16[1,16,32,512]{3,2,1,0:T(8,128)(2,1)S(1)}, bf16[1,16,32,512]{3,2,1,0:T(8,128)(2,1)}, u32[]{:S(2)}) copy-start(bf16[1,16,32,512]{3,2,1,0:T(8,128)(2,1)} %param.26) | copy-start | bytes 1572868
  131.3 19.2 %copy-start.15 = (f32[1,16,32,512]{3,1,2,0:T(8,128)S(1)}, f32[1,16,32,512]{3,1,2,0:T(8,128)}, u32[]{:S(2)}) copy-start(f32[1,16,32,512]{3,1,2,0:T(8,128)} %get-tuple-element.98) | copy-start | bytes 3145732
  131.3 19.2 %copy-start.66 = (f32[1,512]{1,0:T(1,128)S(1)}, f32[1,512]{1,0:T(1,128)}, u32[]{:S(2)}) copy-start(f32[1,512]{1,0:T(1,128)} %copy-done.65) | copy-start | bytes 6148
  166.1 154.2 %reduce-scatter.8.cloned.1.call-start = ((), (), s32[]{:S(2)}) async-start(), calls=%async_computation.6 | async-start | bytes 5013504 | tf_op jit(solution)/shard_map/reduce_scatter | solution.py:310
  167.2 4.1 collective-permute-start.4
  169.4 6.2 %collective-permute-start.5 = (bf16[1,1,32,512]{3,1,2,0:T(2,128)(2,1)S(1)}, bf16[1,1,32,512]{3,1,2,0:T(2,128)(2,1)S(1)}, u32[]{:S(2)}, u32[]{:S(2)}) collective-permute-start(bf16[1,1,32,512]{3,1,2,0:T(2,128)(2,1)S(1)} %get-tuple-element.107), channel_id=1, source_target_pairs={{1,0},{3,2},{5,4},{7,6},{9,8},{11,10},{13,12},{15,14},{17,16},{19,... | collective-permute-start | bytes 98312 | tf_op jit(solution)/shard_map/ppermute | solution.py:19
  200.8 41.0 %copy-start.22 = (bf16[512,256]{1,0:T(8,128)(2,1)S(1)}, bf16[512,256]{1,0:T(8,128)(2,1)}, u32[]{:S(2)}) copy-start(bf16[512,256]{1,0:T(8,128)(2,1)} %copy-done.21) | copy-start | bytes 786436
  200.8 42.9 %copy-start.24 = (bf16[8,32,512]{2,1,0:T(8,128)(2,1)S(1)}, bf16[8,32,512]{2,1,0:T(8,128)(2,1)}, u32[]{:S(2)}) copy-start(bf16[8,32,512]{2,1,0:T(8,128)(2,1)} %copy-done.23) | copy-start | bytes 786436
  200.8 43.9 %copy-start.64 = (f32[256]{0:T(256)S(1)}, f32[256]{0:T(256)}, u32[]{:S(2)}) copy-start(f32[256]{0:T(256)} %param.43) | copy-start | bytes 3076
  200.9 43.9 %copy-start.70 = (f32[256]{0:T(256)S(1)}, f32[256]{0:T(256)}, u32[]{:S(2)}) copy-start(f32[256]{0:T(256)} %param.44) | copy-start | bytes 3076
  200.9 179.3 %reduce-scatter.14.cloned.1.call-start = ((), (), s32[]{:S(2)}) async-start(), calls=%async_computation.9 | async-start | bytes 442368 | tf_op jit(solution)/shard_map/reduce_scatter | solution.py:321
  204.4 40.3 %copy-start.6 = (f32[512,256]{1,0:T(8,128)S(1)}, f32[512,256]{1,0:T(8,128)}, u32[]{:S(2)}) copy-start(f32[512,256]{1,0:T(8,128)} %copy-done.5) | copy-start | bytes 1572868
  241.8 140.0 %reduce-scatter.10.cloned.1.call-start = ((), (), s32[]{:S(2)}) async-start(), calls=%async_computation.7 | async-start | bytes 442368 | tf_op jit(solution)/shard_map/reduce_scatter | solution.py:318
  244.7 75.7 %copy-start.16 = (bf16[512,1,512]{0,2,1:T(8,128)(2,1)S(1)}, bf16[512,1,512]{0,2,1:T(8,128)(2,1)}, u32[]{:S(2)}) copy-start(bf16[512,1,512]{0,2,1:T(8,128)(2,1)} %reduce-scatter.6.cloned.1.call-done) | copy-start | bytes 1572868
  244.7 76.6 %copy-start.4 = (f32[512,256]{1,0:T(8,128)S(1)}, f32[512,256]{1,0:T(8,128)}, u32[]{:S(2)}) copy-start(f32[512,256]{1,0:T(8,128)} %copy-done.2) | copy-start | bytes 1572868
  248.6 73.7 %copy-start.13 = (bf16[1,16,32,512]{3,2,1,0:T(8,128)(2,1)S(1)}, bf16[1,16,32,512]{3,2,1,0:T(8,128)(2,1)}, u32[]{:S(2)}) copy-start(bf16[1,16,32,512]{3,2,1,0:T(8,128)(2,1)} %copy-done.12) | copy-start | bytes 1572868
  248.6 73.7 %copy-start.28 = (bf16[512,256]{1,0:T(8,128)(2,1)S(1)}, bf16[512,256]{1,0:T(8,128)(2,1)}, u32[]{:S(2)}) copy-start(bf16[512,256]{1,0:T(8,128)(2,1)} %copy-done.27) | copy-start | bytes 786436
  320.3 192.0 %all-reduce.6.cloned.1.call-start = ((), (), s32[]{:S(2)}) async-start(), calls=%async_computation.10 | async-start | bytes 11534336 | tf_op jit(solution)/shard_map/psum | solution.py:325
  323.5 48.1 %copy-start.37 = (bf16[16,1,32,512]{3,0,2,1:T(8,128)(2,1)S(1)}, bf16[16,1,32,512]{3,0,2,1:T(8,128)(2,1)}, u32[]{:S(2)}) copy-start(bf16[16,1,32,512]{3,0,2,1:T(8,128)(2,1)} %copy-done.36) | copy-start | bytes 1572868
  323.6 49.2 %slice-start = ((s8[4718592]{0:T(1024)(128)(4,1)}), s8[524288]{0:T(1024)(128)(4,1)S(1)}, s32[]{:S(2)}) async-start(s8[4718592]{0:T(1024)(128)(4,1)} %bitcast.521), calls=%async_computation.11 | async-start | bytes 1048576
  325.5 46.4 %collective-permute-start.6 = (bf16[1,1,32,512]{3,2,1,0:T(8,128)(2,1)S(1)}, bf16[1,1,32,512]{3,2,1,0:T(8,128)(2,1)S(1)}, u32[]{:S(2)}, u32[]{:S(2)}) collective-permute-start(bf16[1,1,32,512]{3,2,1,0:T(8,128)(2,1)S(1)} %slice.166), channel_id=1, source_target_pairs={{0,1},{2,3},{4,5},{6,7},{8,9},{10,11},{12,13},{14,15},{16,17},{18,... | collective-permute-start | bytes 98312 | tf_op jit(solution)/shard_map/ppermute | solution.py:16
  328.9 43.0 %collective-permute-start.7 = (bf16[1,1,32,512]{3,2,1,0:T(8,128)(2,1)S(1)}, bf16[1,1,32,512]{3,2,1,0:T(8,128)(2,1)S(1)}, u32[]{:S(2)}, u32[]{:S(2)}) collective-permute-start(bf16[1,1,32,512]{3,2,1,0:T(8,128)(2,1)S(1)} %slice.169), channel_id=1, source_target_pairs={{1,0},{3,2},{5,4},{7,6},{9,8},{11,10},{13,12},{15,14},{17,16},{19,... | collective-permute-start | bytes 98312 | tf_op jit(solution)/shard_map/ppermute | solution.py:19
  (74 other events, 269.4 us)
Sparse Core Ops, SparseCore 0:
  124.0 22.9 reduce-scatter.5
  166.2 75.5 reduce-scatter.11
  245.6 74.6 reduce-scatter.7
  322.5 11.4 reduce-scatter.13
  336.1 12.5 reduce-scatter.9
  357.3 154.9 all-reduce.5
where the time goes:
time: 539 us; the launch traced here: 531 us
  waiting for transfers between devices  258 us (48%)
  matrix products  116 us (22%)
  blocking collectives  60.7 us (11%)
  local copies, waits for them, and re-layouts  38 us (7%)
  other arithmetic  22.4 us (4%)
  between operations  17.9 us (3%)
  starting transfers between devices  17.5 us (3%)
    psum x1, waiting for transfers between devices, body(): lax.psum((project_weight_grad, project_bias_grad, query_weight_grad, quer...  129 us
    reduce_scatter x1, waiting for transfers between devices, body(): lax.psum_scatter(first_kernel_grad.astype(jnp.bfloat16), 'page', scatter_...  71.7 us
    psum x1, blocking collectives, body(): lax.psum((project_weight_grad, project_bias_grad, query_weight_grad, quer...  41.2 us
    reduce_scatter x1, waiting for transfers between devices, body(): lax.psum_scatter(second_kernel_grad.astype(jnp.bfloat16), 'page', scatter...  37.4 us
    unnamed x199, local copies, waits for them, and re-layouts  27.7 us
    dot_general x18, matrix products, kernel_grad(): jnp.einsum('prci,prco->io', window, upstream, preferred_element_type=jnp....  26.5 us
    conv_general_dilated x4, matrix products, conv_valid(): lax.conv_general_dilated(padded, kernel, (1, 1), 'VALID', dimension_numbe...  24.3 us
    reduce_scatter x1, waiting for transfers between devices, body(): lax.psum_scatter(jnp.concatenate([key_part.reshape(length * lax.axis_size...  15.7 us
  transfers between devices with their start and end apart: 14, of which 6 were waited for; matrix products, arithmetic and copies ran while one was open for 11% of the time, Pallas kernels for 0%

commit v1 on v0

--- a/solution.py
+++ b/solution.py
@@ -1,8 +1,11 @@
+import functools
 import math
 
 import jax
 import jax.numpy as jnp
 from jax import lax
+from jax.experimental import pallas as pl
+from jax.experimental.pallas import tpu as pltpu
 from jax.sharding import PartitionSpec as P
 
 HEADS = 8
@@ -347,9 +350,758 @@
     return (encoded, features_grad, first_part, second_part) + tuple(dense)
 
 
+MESH = pl.DeviceIdType.MESH
+STEPS = {"core": 1, "y": 2, "z0": 4, "z1": 8}
+ORDERS = (("x", "y", "z0", "z1"), ("y", "x", "z0", "z1"), ("z0", "z1", "x", "y"))
+
+
+def own_bits():
+    page, strip = lax.axis_index("page"), lax.axis_index("strip")
+    bits = {name: (page // step) % 2 for name, step in STEPS.items()}
+    peers = {name: (page + step - 2 * step * bits[name], strip) for name, step in STEPS.items()}
+    bits["x"] = strip
+    peers["x"] = (page, 1 - strip)
+    peers["across"] = (peers["core"][0], 1 - strip)
+    return bits, peers
+
+
+def enter(peers):
+    barrier = pltpu.get_barrier_semaphore()
+    for peer in peers.values():
+        pl.semaphore_signal(barrier, inc=1, device_id=peer, device_id_type=MESH)
+    pl.semaphore_wait(barrier, len(peers))
+
+
+def remote(source, target, sends, recvs, peer):
+    return pltpu.make_async_remote_copy(
+        source, target, sends, recvs, device_id=peer, device_id_type=MESH
+    )
+
+
+def slot_of(order, place):
+    slot = 0
+    for name in order:
+        slot = slot * 2 + place[name]
+    return slot
+
+
+class Halving:
+    def __init__(self, order, bits, peers, current, parts, sums, sends, recvs, whole=None):
+        self.order, self.bits, self.peers = order, bits, peers
+        self.current, self.parts, self.sums = current, parts, sums
+        self.sends, self.recvs, self.whole = sends, recvs, whole
+        self.slots = 2 ** len(order)
+        self.flight = None
+
+    def steps(self):
+        return len(self.order) * (1 if self.whole is None else 2)
+
+    def begin(self, step):
+        count = len(self.order)
+        if step < count:
+            name = self.order[step]
+            half = self.slots >> (step + 1)
+            offset = self.slots - (self.slots >> step)
+            source = self.current.at[pl.ds((1 - self.bits[name]) * half, half)]
+            target = self.parts.at[pl.ds(offset, half)]
+        else:
+            level = 2 * count - 1 - step
+            name = self.order[level]
+            size = self.slots >> (level + 1)
+            first = 0
+            for depth in range(level + 1):
+                first = first + self.bits[self.order[depth]] * (self.slots >> (depth + 1))
+            source = self.whole.at[pl.ds(first, size)]
+            target = self.whole.at[pl.ds(first, size)]
+        self.flight = remote(
+            source, target, self.sends.at[step], self.recvs.at[step], self.peers[name]
+        )
+        self.flight.start()
+
+    def end(self, step):
+        count = len(self.order)
+        self.flight.wait()
+        if step >= count:
+            return None
+        name = self.order[step]
+        half = self.slots >> (step + 1)
+        offset = self.slots - (self.slots >> step)
+        mine = self.current[pl.ds(self.bits[name] * half, half)]
+        total = mine.astype(jnp.float32) + self.parts[pl.ds(offset, half)].astype(jnp.float32)
+        if step == count - 1:
+            return total
+        following = self.sums.at[pl.ds(offset, half)]
+        following[...] = total.astype(jnp.bfloat16)
+        self.current = following
+        return None
+
+
+def link_plan(units):
+    waiting = sorted((ready, unit, 0) for unit, (ready, _) in enumerate(units))
+    free, finished = {}, []
+    while waiting:
+        ready, unit, step = waiting.pop(0)
+        link, spent = units[unit][1][step]
+        begin = max(ready, free.get(link, 0.0))
+        free[link] = begin + spent
+        done = begin + spent + 1.5
+        finished.append((done, unit, step))
+        if step + 1 < len(units[unit][1]):
+            waiting.append((done, unit, step + 1))
+            waiting.sort()
+    return sorted(finished)
+
+
+def link_costs(order, size, back):
+    costs = []
+    for name in order:
+        size = size / 2
+        if name == "core":
+            costs.append(("core", size / 6e5))
+        else:
+            costs.append((name[0], size * (4 if name == "z1" else 2) / 1e5))
+    return costs + costs[::-1] if back else costs
+
+
+def shifted(value):
+    side = value.shape[0]
+    wide = value.astype(jnp.float32)
+    column = lax.broadcasted_iota(jnp.int32, wide.shape, 0)
+    later = jnp.where(column < side - 1, pltpu.roll(wide, side - 1, 0), 0.0)
+    earlier = jnp.where(column > 0, pltpu.roll(wide, 1, 0), 0.0)
+    return later.astype(jnp.bfloat16), earlier.astype(jnp.bfloat16)
+
+
+def late_kernel(
+    side,
+    late_ref,
+    slope_ref,
+    direct_ref,
+    hidden_ref,
+    features_ref,
+    first_hbm,
+    second_hbm,
+    dense_ref,
+    small_ref,
+    fgrad_ref,
+    first_out,
+    second_out,
+    dense_out,
+    small_out,
+    first_w,
+    second_w,
+    hidden_all,
+    features_all,
+    late_ext,
+    late_side,
+    late_pair,
+    late_sib,
+    early_side,
+    early_pair,
+    early_sib,
+    grads,
+    parts,
+    sums,
+    dense_parts,
+    dense_sums,
+    small_parts,
+    small_sums,
+    owned,
+    owned_sib,
+    weight_sems,
+    pair_sends,
+    pair_recvs,
+    grad_sends,
+    grad_recvs,
+    dense_sends,
+    dense_recvs,
+    small_sends,
+    small_recvs,
+    owned_sends,
+    owned_recvs,
+):
+    length, channels = late_ref.shape
+    rows = length // side
+    lanes = 128
+    bits, peers = own_bits()
+    strip, core = bits["x"], bits["core"]
+    second_load = pltpu.make_async_copy(second_hbm, second_w, weight_sems.at[0])
+    first_load = pltpu.make_async_copy(first_hbm, first_w, weight_sems.at[1])
+    second_load.start()
+    first_load.start()
+    enter(peers)
+
+    edge = 2 * side
+    own_edge = (1 - strip) * (length - edge)
+    halo_at = strip * (length + edge)
+    copies = [
+        remote(
+            late_ref.at[pl.ds(pl.multiple_of(own_edge, side), edge)],
+            late_ext.at[pl.ds(pl.multiple_of(halo_at, side), edge)],
+            pair_sends.at[0],
+            pair_recvs.at[0],
+            peers["x"],
+        )
+    ]
+    number = 1
+    for part in range(2):
+        chunk = pl.ds(pl.multiple_of(part * 2 * lanes + (1 - core) * lanes, lanes), lanes)
+        copies.append(
+            remote(
+                late_ref.at[:, chunk],
+                late_sib.at[pl.ds(side, length), pl.ds(part * lanes, lanes)],
+                pair_sends.at[number],
+                pair_recvs.at[number],
+                peers["core"],
+            )
+        )
+        copies.append(
+            remote(
+                late_ref.at[pl.ds(pl.multiple_of((1 - strip) * (length - side), side), side), chunk],
+                late_sib.at[
+                    pl.ds(pl.multiple_of(strip * (length + side), side), side),
+                    pl.ds(part * lanes, lanes),
+                ],
+                pair_sends.at[number + 1],
+                pair_recvs.at[number + 1],
+                peers["across"],
+            )
+        )
+        number += 2
+    for source, target in ((hidden_ref, hidden_all), (features_ref, features_all)):
+        copies.append(
+            remote(
+                source,
+                target.at[1],
+                pair_sends.at[number],
+                pair_recvs.at[number],
+                peers["core"],
+            )
+        )
+        number += 1
+    for copy in copies:
+        copy.start()
+
+    dense_units = dense_ref.shape[0]
+    taps = 9
+    reducers, costs = [], []
+    for unit in range(dense_units):
+        order = ("core",) + ORDERS[unit % 2]
+        reducers.append(
+            Halving(
+                order,
+                bits,
+                peers,
+                dense_ref.at[unit],
+                dense_parts.at[unit],
+                dense_sums.at[unit],
+                dense_sends.at[unit],
+                dense_recvs.at[unit],
+                dense_out.at[unit],
+            )
+        )
+        costs.append((1.0, link_costs(order, 262144, True)))
+    for unit in range(2 * taps):
+        order = ORDERS[(0, 1, 0, 1, 2, 0, 1, 0, 1)[unit % taps]]
+        reducers.append(
+            Halving(
+                order,
+                bits,
+                peers,
+                grads.at[unit],
+                parts.at[unit],
+                sums.at[unit],
+                grad_sends.at[unit],
+                grad_recvs.at[unit],
+            )
+        )
+        made = 4.0 + 0.5 * unit if unit < taps else 14.0 + 0.5 * (unit - taps)
+        costs.append((made, link_costs(order, 262144, False)))
+    agenda = link_plan(costs)
+
+    def advance(now):
+        while agenda and agenda[0][0] <= now:
+            _, unit, step = agenda.pop(0)
+            reducer = reducers[unit]
+            total = reducer.end(step)
+            if total is not None:
+                low = total.astype(jnp.bfloat16)
+                if unit < dense_units:
+                    place = 0
+                    for name in reducer.order:
+                        place = place * 2 + bits[name]
+                    dense_out[unit, pl.ds(place, 1)] = low
+                else:
+                    tap = unit - dense_units
+                    owned[tap // taps, 0, tap % taps] = low[0, : low.shape[1] // 2]
+                    owned[tap // taps, 1, tap % taps] = low[0, low.shape[1] // 2 :]
+            if step + 1 < reducer.steps():
+                reducer.begin(step + 1)
+
+    for unit in range(dense_units):
+        reducers[unit].begin(0)
+
+    blank = jnp.zeros((edge, channels), jnp.bfloat16)
+    late_ext[pl.ds(pl.multiple_of(strip * (length + edge), side), edge)] = blank
+    late_sib[pl.ds(pl.multiple_of(strip * (length + side), side), side)] = blank[
+        :side, : 2 * lanes
+    ]
+    late_ext[pl.ds(edge, length)] = late_ref[...]
+    hidden_all[0] = hidden_ref[...]
+    features_all[0] = features_ref[...]
+    small_now = small_ref[...]
+    for step, name in enumerate(("core", "x", "y", "z0", "z1")):
+        small_sums[step] = small_now
+        copy = remote(
+            small_sums.at[step],
+            small_parts.at[step],
+            small_sends.at[step],
+            small_recvs.at[step],
+            peers[name],
+        )
+        copy.start()
+        copy.wait()
+        small_now = small_now + small_parts[step]
+    small_out[...] = small_now
+    for copy in copies:
+        copy.wait()
+
+    def spread(source, target, chunk, count):
+        def one(row, carry):
+            at = pl.ds(pl.multiple_of(row * side, side), side)
+            value = source[at] if chunk is None else source[at, chunk]
+            later, earlier = shifted(value)
+            if chunk is None:
+                target[0, at] = later
+                target[1, at] = value
+                target[2, at] = earlier
+            else:
+                lane = chunk[1]
+                target[0, at, lane] = later
+                target[1, at, lane] = value
+                target[2, at, lane] = earlier
+            return carry
+
+        lax.fori_loop(0, count, one, 0)
+
+    def spread_pair(source, target, skip):
+        def one(row, carry):
+            at = pl.ds(pl.multiple_of(row * side, side), side)
+            for part in range(2):
+                chunk = pl.ds(pl.multiple_of(part * 2 * lanes + core * lanes, lanes), lanes)
+                value = source[pl.ds(pl.multiple_of((row + skip) * side, side), side), chunk]
+                later, earlier = shifted(value)
+                lane = pl.ds(part * lanes, lanes)
+                target[0, at, lane] = later
+                target[1, at, lane] = value
+                target[2, at, lane] = earlier
+            return carry
+
+        lax.fori_loop(0, rows + 2, one, 0)
+
+    def kernel_grads(left, own, sibling, first_unit, clock):
+        for tap in range(taps):
+            down, across = tap // 3, tap % 3
+            window = pl.ds(side * (2 - down), length)
+            product = jnp.dot(
+                left[0], own[0 + across, window], preferred_element_type=jnp.float32
+            ) + jnp.dot(left[1], sibling[across, window], preferred_element_type=jnp.float32)
+            low = product.astype(jnp.bfloat16)
+            unit = first_unit + tap
+            order = reducers[dense_units + unit].order
+            block = low.shape[0] // 8
+            for chip in range(8):
+                for half in range(2):
+                    slot = slot_of(
+                        order,
+                        {"x": half, "y": chip % 2, "z0": chip // 2 % 2, "z1": chip // 4},
+                    )
+                    grads[unit, slot] = low[
+                        chip * block : (chip + 1) * block, half * lanes : (half + 1) * lanes
+                    ]
+            reducers[dense_units + unit].begin(0)
+            advance(clock + 0.5 * tap)
+
+    spread(late_ext, late_side, None, rows + 4)
+    spread_pair(late_ext, late_pair, 1)
+    spread(late_sib, early_sib, None, rows + 2)
+    kernel_grads(hidden_all, late_pair, early_sib, 0, 4.0)
+    second_load.wait()
+
+    def transposed_conv(shifts, weight, count):
+        total = None
+        for tap in range(taps):
+            down, across = tap // 3, tap % 3
+            term = lax.dot_general(
+                shifts[across, pl.ds(side * (2 - down), count)],
+                weight[tap],
+                (((1,), (1,)), ((), ())),
+                preferred_element_type=jnp.float32,
+            )
+            total = term if total is None else total + term
+        return total
+
+    early = (transposed_conv(late_side, second_w, length + edge) * slope_ref[...]).astype(
+        jnp.bfloat16
+    )
+    early_side[1] = early
+    pair_copies = []
+    for part in range(2):
+        chunk = pl.ds(pl.multiple_of(part * 2 * lanes + (1 - core) * lanes, lanes), lanes)
+        pair_copies.append(
+            remote(
+                early_side.at[1, :, chunk],
+                early_pair.at[:, pl.ds(part * lanes, lanes)],
+                pair_sends.at[number],
+                pair_recvs.at[number],
+                peers["core"],
+            )
+        )
+        number += 1
+    for copy in pair_copies:
+        copy.start()
+    advance(10.0)
+    spread(early_side.at[1], late_side, None, rows + 2)
+    spread_pair(early_side.at[1], late_pair, 0)
+    for copy in pair_copies:
+        copy.wait()
+    spread(early_pair, early_sib, None, rows + 2)
+    kernel_grads(features_all, late_pair, early_sib, taps, 14.0)
+    first_load.wait()
+    fgrad_ref[...] = transposed_conv(late_side, first_w, length) + direct_ref[...]
+    advance(1e9)
+    finals = []
+    for which, out in ((1, first_out), (0, second_out)):
+        copy = remote(
+            owned.at[which, 1 - core],
+            owned_sib.at[which],
+            owned_sends.at[which],
+            owned_recvs.at[which],
+            peers["core"],
+        )
+        copy.start()
+        finals.append((copy, which, out))
+    for copy, which, out in finals:
+        copy.wait()
+        out[:, :, pl.ds(pl.multiple_of(core * lanes, lanes), lanes)] = owned[which, core].astype(
+            jnp.float32
+        )
+        out[:, :, pl.ds(pl.multiple_of((1 - core) * lanes, lanes), lanes)] = owned_sib[
+            which
+        ].astype(jnp.float32)
+
+
+def late_call(side, late, slope, direct, hidden, features, first, second, dense, small):
+    length, channels = late.shape
+    edge = 2 * side
+    units = dense.shape[0]
+    bf16, f32 = jnp.bfloat16, jnp.float32
+    vmem = pl.BlockSpec(memory_space=pltpu.VMEM)
+    hbm = pl.BlockSpec(memory_space=pl.ANY)
+    sems = pltpu.SemaphoreType.DMA
+    return pl.pallas_call(
+        functools.partial(late_kernel, side),
+        out_shape=(
+            jax.ShapeDtypeStruct((length, channels), f32),
+            jax.ShapeDtypeStruct((9, channels // 16, channels // 2), f32),
+            jax.ShapeDtypeStruct((9, channels // 16, channels // 2), f32),
+            jax.ShapeDtypeStruct(dense.shape, bf16),
+            jax.ShapeDtypeStruct(small.shape, f32),
+        ),
+        in_specs=[vmem] * 5 + [hbm] * 2 + [vmem] * 2,
+        out_specs=[vmem] * 5,
+        scratch_shapes=[
+            pltpu.VMEM(first.shape, bf16),
+            pltpu.VMEM(second.shape, bf16),
+            pltpu.VMEM((2, channels, length), bf16),
+            pltpu.VMEM((2, channels, length), bf16),
+            pltpu.VMEM((length + 2 * edge, channels), bf16),
+            pltpu.VMEM((3, length + 2 * edge, channels), bf16),
+            pltpu.VMEM((3, length + edge, channels // 2), bf16),
+            pltpu.VMEM((length + edge, channels // 2), bf16),
+            pltpu.VMEM((3, length + edge, channels), bf16),
+            pltpu.VMEM((length + edge, channels // 2), bf16),
+            pltpu.VMEM((3, length + edge, channels // 2), bf16),
+            pltpu.VMEM((18, 16, channels // 8, 128), bf16),
+            pltpu.VMEM((18, 16, channels // 8, 128), bf16),
+            pltpu.VMEM((18, 16, channels // 8, 128), bf16),
+            pltpu.VMEM(dense.shape, bf16),
+            pltpu.VMEM(dense.shape, bf16),
+            pltpu.VMEM((5,) + small.shape, f32),
+            pltpu.VMEM((5,) + small.shape, f32),
+            pltpu.VMEM((2, 2, 9, channels // 16, 128), bf16),
+            pltpu.VMEM((2, 9, channels // 16, 128), bf16),
+            sems((2,)),
+            sems((9,)),
+            sems((9,)),
+            sems((18, 4)),
+            sems((18, 4)),
+            sems((units, 10)),
+            sems((units, 10)),
+            sems((5,)),
+            sems((5,)),
+            sems((2,)),
+            sems((2,)),
+        ],
+        compiler_params=pltpu.CompilerParams(
+            collective_id=0, has_side_effects=True, vmem_limit_bytes=62 * 1024 * 1024
+        ),
+        name="late_gradients",
+    )(late, slope, direct, hidden, features, first, second, dense, small)
+
+
+def swap(value):
+    return lax.ppermute(value, "strip", [(0, 1), (1, 0)])
+
+
+def gelu_both(value):
+    bell = 0.5 * (1.0 + lax.erf(value * math.sqrt(0.5)))
+    density = jnp.exp(-0.5 * value * value) * (1.0 / math.sqrt(2.0 * math.pi))
+    return value * bell, bell + value * density
+
+
+def paired_body(
+    features,
+    quarter_turns,
+    heights,
+    widths,
+    frozen_scale,
+    frozen_shift,
+    first_kernel,
+    second_kernel,
+    project_weight,
+    project_bias,
+    query_weight,
+    query_bias,
+    key_weight,
+    value_weight,
+    value_bias,
+    output_weight,
+    output_bias,
+    first_gain,
+    first_shift,
+    expand_weight,
+    expand_bias,
+    shrink_weight,
+    shrink_bias,
+    final_gain,
+    final_shift,
+    cotangent,
+):
+    pages, rows, side, channels = features.shape
+    width = project_weight.shape[1]
+    head_size = width // HEADS
+    length = rows * side
+    strip = lax.axis_index("strip")
+    row_start = strip * rows
+    factor = head_size ** (-0.5)
+
+    got = swap(lax.dynamic_slice_in_dim(features, (1 - strip) * (rows - 2), 2, axis=1))
+    extended = jnp.concatenate(
+        [
+            jnp.where(strip == 1, got, jnp.zeros_like(got)),
+            features,
+            jnp.where(strip == 0, got, jnp.zeros_like(got)),
+        ],
+        axis=1,
+    )
+    first_pre = (
+        conv_valid(pad_columns(extended), first_kernel) * frozen_scale[0] + frozen_shift[0]
+    )
+    place = row_start - 1 + jnp.arange(rows + 2)
+    inside = ((place >= 0) & (place < 2 * rows))[None, :, None, None]
+    hidden, slope = gelu_both(first_pre)
+    hidden = jnp.where(inside, hidden, 0.0).astype(jnp.bfloat16)
+    slope = jnp.where(inside, slope * frozen_scale[0], 0.0)
+    second_pre = (
+        conv_valid(pad_columns(hidden), second_kernel) * frozen_scale[1]
+        + frozen_shift[1]
+        + features.astype(jnp.float32)
+    )
+    block, second_slope = gelu_both(second_pre.reshape(length, channels))
+    block = block.astype(jnp.bfloat16)
+    source = jnp.dot(block, project_weight, preferred_element_type=jnp.float32) + project_bias
+    position, valid = sine_positions(quarter_turns, heights, widths, row_start, rows, side, width)
+    other_valid = sine_positions(
+        quarter_turns, heights, widths, (1 - strip) * rows, rows, side, width
+    )[1]
+    joint = (source + position.reshape(length, width)).astype(jnp.bfloat16)
+    plain = source.astype(jnp.bfloat16)
+    queries = (
+        jnp.dot(joint, query_weight, preferred_element_type=jnp.float32) + query_bias
+    ).astype(jnp.bfloat16)
+    queries = queries.reshape(length, HEADS, head_size)
+    keys_own = jnp.dot(joint, key_weight, preferred_element_type=jnp.float32).astype(jnp.bfloat16)
+    values_own = (
+        jnp.dot(plain, value_weight, preferred_element_type=jnp.float32) + value_bias
+    ).astype(jnp.bfloat16)
+    pair = jnp.concatenate([keys_own, values_own], axis=1)
+    pair = jnp.concatenate([pair, swap(pair)], axis=0)
+    keys_four = pair[:, :width].reshape(2 * length, HEADS, head_size)
+    values_four = pair[:, width:].reshape(2 * length, HEADS, head_size)
+    key_bias = jnp.where(
+        jnp.concatenate([valid.reshape(length), other_valid.reshape(length)]), 0.0, -10000.0
+    )
+    scores = jnp.einsum("qhd,khd->hqk", queries, keys_four, preferred_element_type=jnp.float32)
+    scores = scores * factor + key_bias
+    peak = jnp.max(scores, axis=-1)
+    expd = jnp.exp(scores - peak[..., None])
+    denom = jnp.sum(expd, axis=-1)
+    logsum = peak + jnp.log(denom)
+    low_prob = (expd / denom[..., None]).astype(jnp.bfloat16)
+    mixed = jnp.einsum("hqk,khd->qhd", low_prob, values_four, preferred_element_type=jnp.float32)
+    combined = mixed.reshape(length, width).astype(jnp.bfloat16)
+    attended = jnp.dot(combined, output_weight, preferred_element_type=jnp.float32) + output_bias
+    first_sum = source + attended
+    normed = layer_norm(first_sum, first_gain, first_shift)
+    ff_in = normed.astype(jnp.bfloat16)
+    expanded = jnp.dot(ff_in, expand_weight, preferred_element_type=jnp.float32) + expand_bias
+    activated = gelu_exact(expanded).astype(jnp.bfloat16)
+    second_sum = (
+        normed + jnp.dot(activated, shrink_weight, preferred_element_type=jnp.float32) + shrink_bias
+    )
+    result, final_back = jax.vjp(layer_norm, second_sum, final_gain, final_shift)
+    encoded = result.astype(jnp.bfloat16).reshape(pages, rows, side, width)
+    d_second, final_gain_grad, final_shift_grad = final_back(
+        cotangent.astype(jnp.float32).reshape(length, width)
+    )
+    d_shrunk = d_second.astype(jnp.bfloat16)
+    shrink_bias_grad = column_sum(d_shrunk)
+    shrink_weight_grad = left_product(activated, d_shrunk)
+    d_expanded = gelu_back(expanded, right_back(d_shrunk, shrink_weight)).astype(jnp.bfloat16)
+    expand_bias_grad = column_sum(d_expanded)
+    expand_weight_grad = left_product(ff_in, d_expanded)
+    d_normed = right_back(d_expanded, expand_weight) + d_second
+    d_first, first_gain_grad, first_shift_grad = jax.vjp(
+        layer_norm, first_sum, first_gain, first_shift
+    )[1](d_normed)
+    d_attended = d_first.astype(jnp.bfloat16)
+    output_bias_grad = column_sum(d_attended)
+    output_weight_grad = left_product(combined, d_attended)
+    d_combined = lax.optimization_barrier(
+        right_back(d_attended, output_weight).astype(jnp.bfloat16)
+    ).reshape(length, HEADS, head_size)
+    delta = jnp.sum(d_combined.astype(jnp.float32) * mixed, axis=-1).T
+    prob = jnp.exp(scores - logsum[..., None])
+    d_prob = jnp.einsum("qhd,khd->hqk", d_combined, values_four, preferred_element_type=jnp.float32)
+    d_scores = (prob * (d_prob - delta[..., None])).astype(jnp.bfloat16)
+    weights_low = prob.astype(jnp.bfloat16)
+    d_queries = factor * jnp.einsum(
+        "hqk,khd->qhd", d_scores, keys_four, preferred_element_type=jnp.float32
+    )
+    key_part = factor * jnp.einsum(
+        "hqk,qhd->khd", d_scores, queries, preferred_element_type=jnp.float32
+    )
+    value_part = jnp.einsum(
+        "hqk,qhd->khd", weights_low, d_combined, preferred_element_type=jnp.float32
+    )
+    both = jnp.concatenate(
+        [key_part.reshape(2 * length, width), value_part.reshape(2 * length, width)], axis=1
+    )
+    summed = both[:length] + swap(both[length:].astype(jnp.bfloat16)).astype(jnp.float32)
+    d_queries_low = d_queries.reshape(length, width).astype(jnp.bfloat16)
+    d_keys_low = summed[:, :width].astype(jnp.bfloat16)
+    d_values_low = summed[:, width:].astype(jnp.bfloat16)
+    query_bias_grad = column_sum(d_queries_low)
+    query_weight_grad = left_product(joint, d_queries_low)
+    key_weight_grad = left_product(joint, d_keys_low)
+    value_weight_grad = left_product(plain, d_values_low)
+    value_bias_grad = column_sum(d_values_low)
+    d_source = (
+        d_first
+        + right_back(d_queries_low, query_weight)
+        + right_back(d_keys_low, key_weight)
+        + right_back(d_values_low, value_weight)
+    )
+    d_source_low = d_source.astype(jnp.bfloat16)
+    project_bias_grad = column_sum(d_source_low)
+    project_weight_grad = left_product(block, d_source_low)
+    d_second_pre = right_back(d_source_low, project_weight) * second_slope
+    d_late = (d_second_pre * frozen_scale[1]).astype(jnp.bfloat16)
+
+    hidden_units = expand_weight.shape[1]
+    dense = jnp.concatenate(
+        [
+            shrink_weight_grad,
+            jnp.transpose(
+                expand_weight_grad.reshape(width, hidden_units // width, width), (1, 0, 2)
+            ).reshape(hidden_units, width),
+            project_weight_grad,
+            query_weight_grad,
+            key_weight_grad,
+            value_weight_grad,
+            output_weight_grad,
+        ],
+        axis=0,
+    ).astype(jnp.bfloat16)
+    count = dense.shape[0] // 512
+    small_rows = [
+        project_bias_grad,
+        query_bias_grad,
+        value_bias_grad,
+        output_bias_grad,
+        first_gain_grad,
+        first_shift_grad,
+        shrink_bias_grad,
+        final_gain_grad,
+        final_shift_grad,
+    ]
+    small = jnp.concatenate(
+        [jnp.stack(small_rows), expand_bias_grad.reshape(-1, width)], axis=0
+    )
+    small = jnp.pad(small, ((0, -small.shape[0] % 8), (0, 0)))
+    features_grad, first_part, second_part, dense, small = late_call(
+        side,
+        d_late,
+        slope.reshape(-1, channels),
+        d_second_pre,
+        hidden[:, 1:-1].reshape(length, channels).T,
+        features.reshape(length, channels).T,
+        first_kernel.reshape(9, channels, channels),
+        second_kernel.reshape(9, channels, channels),
+        dense.reshape(count, 32, 16, width),
+        small,
+    )
+    dense = dense.reshape(-1, width).astype(jnp.float32)
+    at = 0
+    cut = []
+    for size in (hidden_units, hidden_units, channels, width, width, width, width):
+        cut.append(dense[at : at + size])
+        at += size
+    shrink_sum, expand_sum, project_sum, query_sum, key_sum, value_sum, output_sum = cut
+    expand_sum = jnp.transpose(
+        expand_sum.reshape(hidden_units // width, width, width), (1, 0, 2)
+    ).reshape(width, hidden_units)
+    part_shape = (3, 3, channels // 16, channels // 2)
+    return (
+        encoded,
+        features_grad.reshape(pages, rows, side, channels),
+        first_part.reshape(part_shape),
+        second_part.reshape(part_shape),
+        project_sum,
+        small[0],
+        query_sum,
+        small[1],
+        key_sum,
+        value_sum,
+        small[2],
+        output_sum,
+        small[3],
+        small[4],
+        small[5],
+        expand_sum,
+        small[9 : 9 + hidden_units // width].reshape(hidden_units),
+        shrink_sum,
+        small[6],
+        small[7],
+        small[8],
+    )
+
+
 def solution(mesh):
+    paired = mesh.shape["strip"] == 2 and mesh.shape["page"] == 16
     return jax.shard_map(
-        body,
+        paired_body if paired else body,
         mesh=mesh,
         in_specs=(
             P("page", "strip", None, None),

time: 539 us -> 276 us (0.51)
  waiting for transfers between devices: 258 us -> 8.01 us
  Pallas kernels: 0 us -> 99.1 us
  blocking collectives: 60.7 us -> 0 us
  matrix products: 116 us -> 98.7 us
  starting transfers between devices: 17.5 us -> 3.35 us
  between operations: 17.9 us -> 3.85 us
    psum x1 -> x0, waiting for transfers between devices: 129 us -> none  [body(): lax.psum((project_weight_grad, project_bias_grad, query_weight_grad, quer...]
    reduce_scatter x5 -> x0, waiting for transfers between devices: 125 us -> none  [the longest x1 71.7 us: body(): lax.psum_scatter(first_kernel_grad.astype(jnp.bfloat16), 'page', scatter_...]
    pallas_call x0 -> x1, Pallas kernels: none -> 99.1 us  [late_call(): pl.pallas_call(functools.partial(late_kernel, side), out_shape=(jax.Shape...]
    psum x1 -> x0, blocking collectives: 41.2 us -> none  [body(): lax.psum((project_weight_grad, project_bias_grad, query_weight_grad, quer...]
    dot_general x31 -> x13, matrix products: 70.9 us -> 38.9 us  [the longest x1 9.43 us: paired_body(): jnp.dot(ff_in, expand_weight, preferred_element_type=jnp.float32)]
    all_gather x3 -> x0, blocking collectives: 19.5 us -> none  [the longest x1 7.35 us: body(): values_piece = lax.all_gather(values_local, 'strip', axis=1, tiled=True)]
    conv_general_dilated x4 -> x2, matrix products: 24.3 us -> 42.7 us  [conv_valid(): lax.conv_general_dilated(padded, kernel, (1, 1), 'VALID', dimension_numbe...]
    ppermute x8 -> x3, starting transfers between devices: 17.1 us -> 3.35 us  [swap(): return lax.ppermute(value, 'strip', [(0, 1), (1, 0)])]
  transfers between devices with their start and end apart: 14 -> 3, of which waited for: 6 -> 2; matrix products, arithmetic and copies ran while one was open for 11% -> 9% of each run, Pallas kernels for 0% -> 0%
where the time goes in v1:
time: 276 us; the launch traced here: 272 us
  Pallas kernels  99.1 us (36%)
  matrix products  98.7 us (36%)
  local copies, waits for them, and re-layouts  36 us (13%)
  other arithmetic  22.6 us (8%)
  waiting for transfers between devices  8.01 us (3%)
  between operations  3.85 us (1%)
  starting transfers between devices  3.35 us (1%)
    pallas_call x1, Pallas kernels, late_call(): pl.pallas_call(functools.partial(late_kernel, side), out_shape=(jax.Shape...  99.1 us
    conv_general_dilated x2, matrix products, conv_valid(): lax.conv_general_dilated(padded, kernel, (1, 1), 'VALID', dimension_numbe...  42.7 us
    unnamed x143, local copies, waits for them, and re-layouts  14.8 us
    dot_general x1, matrix products, paired_body(): jnp.dot(ff_in, expand_weight, preferred_element_type=jnp.float32)  9.43 us
    dot_general x7, matrix products, right_back(): jnp.einsum('to,io->ti', upstream, weight, preferred_element_type=jnp.floa...  8.7 us
    dot_general x7, matrix products, left_product(): jnp.einsum('ti,to->io', left, right, preferred_element_type=jnp.float32)  8.36 us
    ppermute x3, waiting for transfers between devices, swap(): return lax.ppermute(value, 'strip', [(0, 1), (1, 0)])  8.01 us
    dot_general x1, matrix products, paired_body(): jnp.einsum('qhd,khd->hqk', d_combined, values_four, preferred_element_typ...  8.01 us
  transfers between devices with their start and end apart: 3, of which 2 were waited for; matrix products, arithmetic and copies ran while one was open for 9% of the time, Pallas kernels for 0%

profile of v1, /device:TPU:0, one launch (start us, length us, event | category | flops | bytes accessed | tf_op | source)
XLA Modules:
  0.0 271.6 jit_solution(3717163985261418051)
XLA Ops:
  0.7 2.1 copy.63
  3.0 3.0 %collective-permute-start = (bf16[1,2,32,512]{3,0,2,1:T(2,128)(2,1)S(1)}, bf16[1,2,32,512]{3,0,2,1:T(2,128)(2,1)S(1)}, u32[]{:S(2)}, u32[]{:S(2)}) collective-permute-start(bf16[1,2,32,512]{3,0,2,1:T(2,128)(2,1)S(1)} %constant_dynamic-slice_fusion), channel_id=1, source_target_pairs={{0,1},{1,0},{2,3},{3,2},{4,5},{5,4},{6,7},{7,6},{8,9},{9,8},{10,11... | collective-permute-start | bytes 196616 | tf_op jit(solution)/shard_map/ppermute | solution.py:854
  11.9 1.9 cosine_select_fusion.1
  14.1 27.2 %broadcast_select_fusion = (f32[1,18,32,512]{3,0,2,1:T(1,128)}, f32[1,18,32,512]{3,0,2,1:T(1,128)S(1)}, f32[1,18,32,512]{3,0,2,1:T(1,128)S(1)}) fusion(pred[18]{0:T(512)(128)(4,1)S(1)} %compare_and_fusion, f32[512]{0:T(512)S(1)} %bitcast.200, f32[512]{0:T(512)S(1)} %bitcast.201, bf16[3,3,512,512]{3,2,1,0:T(8,128)(2,1)} %param.32, ...), kind=kOutput, calls=%fused_computation.31 | convolution fusion | flops 2666790912 | bytes 8917010 | tf_op jit(solution)/shard_map/conv_general_dilated | solution.py:82
  41.3 1.6 fusion.28
  43.0 15.5 %fusion.86 = f32[1,16,32,512]{3,0,2,1:T(1,128)S(1)} fusion(bf16[1,18,32,512]{3,0,2,1:T(2,128)(2,1)S(1)} %fusion.28, bf16[3,3,512,512]{3,2,1,0:T(8,128)(2,1)S(1)} %bitcast.165), kind=kOutput, calls=%fused_computation.194 | convolution fusion | flops 2365587456 | bytes 6356992 | tf_op jit(solution)/shard_map/conv_general_dilated | solution.py:82
  65.5 1.6 convert_reduce_fusion.1
  68.2 2.5 copy.71
  72.1 4.8 %collective-permute-done.1 = bf16[512,512]{0,1:T(8,128)(2,1)} collective-permute-done((bf16[512,512]{0,1:T(8,128)(2,1)}, bf16[512,512]{0,1:T(8,128)(2,1)}, u32[]{:S(2)}, u32[]{:S(2)}) %collective-permute-start.1) | collective-permute-done | bytes 524320 | tf_op jit(solution)/shard_map/ppermute | solution.py:854
  78.1 2.6 fusion.82
  80.7 3.5 %fusion = f32[8,512]{1,0:T(8,128)S(1)} fusion(f32[8,512,1024]{2,1,0:T(8,128)S(1)} %get-tuple-element.84, f32[8,512]{1,0:T(8,128)S(1)} %get-tuple-element.83), kind=kLoop, calls=%fused_computation.5 | loop fusion | flops 8384512 | bytes 16809984 | tf_op jit(solution)/shard_map/reduce_sum | solution.py:949
  84.3 2.2 copy-done.1
  86.5 4.5 %fusion.83 = (bf16[512,8,32]{0,2,1:T(8,128)(2,1)S(1)}, f32[512,8,32]{0,2,1:T(8,128)}) fusion(bf16[1024,8,32]{0,2,1:T(8,128)(2,1)S(1)} %bitcast.179, f32[8,512,1024]{2,1,0:T(8,128)S(1)} %get-tuple-element.84, f32[8,512]{1,0:T(8,128)S(1)} %fusion, f32[8,512]{1,0:T(8,128)S(1)} %get-tuple-element.83), kind=kOutput, calls=%fused_computation.191 | convolution fusion | flops 281149440 | bytes 18120704 | tf_op jit(solution)/shard_map/hqk,khd->qhd/dot_general | solution.py:952
  91.7 9.4 %multiply_convert_fusion.1 = (bf16[512,2048]{1,0:T(8,128)(2,1)S(1)}, f32[512,2048]{1,0:T(8,128)S(1)}, f32[512,2048]{1,0:T(8,128)S(1)}) fusion(f32[2048]{0:T(1024)S(1)} %copy-done.61, bf16[256,2048]{1,0:T(8,128)(2,1)S(1)} %copy-done, f32[512,256]{1,0:T(8,128)S(1)} %get-tuple-element.88, f32[256]{0:T(256)S(1)} %copy-done.47, f32[256]{0:T(256)S(1)} %copy-done.43, ...), kind=kOutput, calls=%fused_computation.14 | convolution fusion | flops 606732288 | bytes 12072960 | tf_op jit(solution)/shard_map/dot_general | solution.py:958
  104.8 3.4 %convert_reduce_fusion = (f32[2048]{0:T(1024)}, bf16[512,2048]{1,0:T(8,128)(2,1)S(1)}) fusion(f32[512,2048]{1,0:T(8,128)S(1)} %get-tuple-element.47, bf16[512,256]{1,0:T(8,128)(2,1)S(1)} %get-tuple-element.37, bf16[2048,256]{1,0:T(8,128)(2,1)S(1)} %copy-done.60, f32[512,2048]{1,0:T(8,128)S(1)} %get-tuple-element.89, f32[2048]{0:T(1024)S(1)} %copy-done.61), kind=kOutput, calls=%fused_computation.12 | convolution fusion | flops 554694656 | bytes 11812864 | tf_op jit(solution)/shard_map/to,io->ti/dot_general | solution.py:113
  109.6 1.8 convolution_convert_fusion
  112.6 1.8 convert_reduce_fusion.3
  115.0 7.3 %fusion.2 = f32[8,32,1024]{2,1,0:T(8,128)S(1)} fusion(bf16[512,8,32]{0,2,1:T(8,128)(2,1)S(1)} %bitcast.166, f32[8,512,1024]{2,1,0:T(8,128)} %copy-done.1, f32[8,512]{1,0:T(8,128)S(1)} %log_add_fusion), kind=kOutput, calls=%fused_computation.7 | convolution fusion | flops 276824064 | bytes 18104320 | tf_op jit(solution)/shard_map/hqk,qhd->khd/dot_general | solution.py:995
  122.3 8.0 %multiply_convert_fusion = bf16[8,512,1024]{2,1,0:T(8,128)(2,1)S(1)} fusion(f32[8,512,1024]{2,1,0:T(8,128)} %copy-done.1, bf16[512,8,32]{0,2,1:T(8,128)(2,1)S(1)} %bitcast.167, bf16[1024,8,32]{0,2,1:T(8,128)(2,1)S(1)} %bitcast.180, f32[8,512]{1,0:T(8,128)S(1)} %bitcast.189, f32[8,512]{1,0:T(8,128)S(1)} %log_add_fusion), kind=kOutput, calls=%fused_computation | convolution fusion | flops 285212672 | bytes 25985024 | tf_op jit(solution)/shard_map/qhd,khd->hqk/dot_general | solution.py:986
  130.3 3.3 %convert_reduce_fusion.5 = (f32[8,32]{1,0:T(8,128)S(1)}, bf16[8,32,512]{2,1,0:T(8,128)(2,1)}) fusion(bf16[1024,8,32]{0,2,1:T(8,128)(2,1)S(1)} %bitcast.161, bf16[8,512,1024]{2,1,0:T(8,128)(2,1)S(1)} %multiply_convert_fusion), kind=kOutput, calls=%fused_computation.117 | convolution fusion | flops 268959488 | bytes 9176064 | tf_op jit(solution)/shard_map/hqk,khd->qhd/dot_general | solution.py:989
  133.7 1.5 convolution_multiply_fusion
  136.4 1.8 fusion.12
  138.9 2.3 copy.82
  141.8 2.3 constant_dynamic-update-slice_fusion
  144.1 1.5 convolution_add_fusion.4
  145.6 3.3 %collective-permute-done.2 = bf16[512,512]{0,1:T(8,128)(2,1)} collective-permute-done((bf16[512,512]{0,1:T(8,128)(2,1)}, bf16[512,512]{0,1:T(8,128)(2,1)}, u32[]{:S(2)}, u32[]{:S(2)}) %collective-permute-start.2) | collective-permute-done | bytes 524320 | tf_op jit(solution)/shard_map/ppermute | solution.py:854
  155.7 1.6 multiply_convert_fusion.2
  158.1 99.1 %late_gradients.1 = (f32[512,512]{1,0:T(8,128)}, f32[9,32,256]{2,1,0:T(8,128)}, f32[9,32,256]{2,1,0:T(8,128)}, bf16[11,32,16,256]{3,2,1,0:T(8,128)(2,1)}, f32[24,256]{1,0:T(8,128)}) custom-call(bf16[512,512]{1,0:T(8,128)(2,1)} %get-tuple-element.93.late_ref, f32[576,512]{1,0:T(8,128)} %bitcast.158, f32[512,512]{1,0:T(8,128)} %get-tuple-element.94.direct_ref, ...), custom_call_target="tpu_custom_call" | custom-call | tf_op jit(solution)/shard_map/late_gradients/pallas_call | solution.py:802
  257.9 1.6 fusion.79
  259.5 1.8 slice.133
  261.3 3.6 %fusion.77 = (f32[4,32,16,256]{3,2,1,0:T(8,128)}, f32[4,32,16,256]{3,2,1,0:T(8,128)S(1)}) fusion(bf16[11,32,16,256]{3,2,1,0:T(8,128)(2,1)} %get-tuple-element.29), kind=kLoop, calls=%fused_computation.185 | loop fusion | bytes 8388608 | tf_op jit(solution)/shard_map/slice | solution.py:1069
  266.3 1.6 copy.74
  (221 shorter events, 37.9 us)
Async XLA Ops:
  0.7 91.0 %copy-start = (bf16[256,2048]{1,0:T(8,128)(2,1)S(1)}, bf16[256,2048]{1,0:T(8,128)(2,1)}, u32[]{:S(2)}) copy-start(bf16[256,2048]{1,0:T(8,128)(2,1)} %param.45) | copy-start | bytes 3145732
  3.0 10.8 %collective-permute-start = (bf16[1,2,32,512]{3,0,2,1:T(2,128)(2,1)S(1)}, bf16[1,2,32,512]{3,0,2,1:T(2,128)(2,1)S(1)}, u32[]{:S(2)}, u32[]{:S(2)}) collective-permute-start(bf16[1,2,32,512]{3,0,2,1:T(2,128)(2,1)S(1)} %constant_dynamic-slice_fusion), channel_id=1, source_target_pairs={{0,1},{1,0},{2,3},{3,2},{4,5},{5,4},{6,7},{7,6},{8,9},{9,8},{10,11... | collective-permute-start | bytes 196616 | tf_op jit(solution)/shard_map/ppermute | solution.py:854
  6.0 36.9 %slice-start = ((s8[4718592]{0:T(1024)(128)(4,1)}), s8[524288]{0:T(1024)(128)(4,1)S(1)}, s32[]{:S(2)}) async-start(s8[4718592]{0:T(1024)(128)(4,1)} %bitcast.164), calls=%async_computation | async-start | bytes 1048576
  8.8 49.7 %copy-start.41 = (f32[1,512]{1,0:T(1,128)}, f32[1,512]{1,0:T(1,128)S(1)}, u32[]{:S(2)}) copy-start(f32[1,512]{1,0:T(1,128)S(1)} %get-tuple-element.74) | copy-start | bytes 6148
  14.0 28.9 %slice-start.1 = ((s8[4718592]{0:T(1024)(128)(4,1)}), s8[4194304]{0:T(1024)(128)(4,1)S(1)}, s32[]{:S(2)}) async-start(s8[4718592]{0:T(1024)(128)(4,1)} %bitcast.164), calls=%async_computation.1 | async-start | bytes 8388608
  42.9 15.6 %copy-start.7 = (bf16[1,16,32,512]{3,2,1,0:T(8,128)(2,1)S(1)}, bf16[1,16,32,512]{3,2,1,0:T(8,128)(2,1)}, u32[]{:S(2)}) copy-start(bf16[1,16,32,512]{3,2,1,0:T(8,128)(2,1)} %param.26) | copy-start | bytes 1572868
  61.3 29.6 %copy-start.5 = (f32[512,256]{1,0:T(8,128)}, f32[512,256]{1,0:T(8,128)S(1)}, u32[]{:S(2)}) copy-start(f32[512,256]{1,0:T(8,128)S(1)} %get-tuple-element.82) | copy-start | bytes 1572868
  63.2 13.7 %collective-permute-start.1 = (bf16[512,512]{0,1:T(8,128)(2,1)}, bf16[512,512]{0,1:T(8,128)(2,1)}, u32[]{:S(2)}, u32[]{:S(2)}) collective-permute-start(bf16[512,512]{0,1:T(8,128)(2,1)} %pad_maximum_fusion.6), channel_id=1, source_target_pairs={{0,1},{1,0},{2,3},{3,2},{4,5},{5,4},{6,7},{7,6},{8,9},{9,8},{10,11... | collective-permute-start | bytes 1572872 | tf_op jit(solution)/shard_map/ppermute | solution.py:854
  63.8 8.1 %copy-start.54 = (f32[256]{0:T(256)S(1)}, f32[256]{0:T(256)}, u32[]{:S(2)}) copy-start(f32[256]{0:T(256)} %param.37) | copy-start | bytes 3076
  64.8 12.1 %copy-start.16 = (bf16[512,256]{0,1:T(8,128)(2,1)S(1)}, bf16[512,256]{0,1:T(8,128)(2,1)}, u32[]{:S(2)}) copy-start(bf16[512,256]{0,1:T(8,128)(2,1)} %copy-done.15) | copy-start | bytes 786436
  64.8 12.1 %copy-start.18 = (bf16[512,256]{0,1:T(8,128)(2,1)S(1)}, bf16[512,256]{0,1:T(8,128)(2,1)}, u32[]{:S(2)}) copy-start(bf16[512,256]{0,1:T(8,128)(2,1)} %copy-done.17) | copy-start | bytes 786436
  72.1 8.6 %copy-start.9 = (bf16[512,256]{0,1:T(8,128)(2,1)}, bf16[512,256]{0,1:T(8,128)(2,1)S(1)}, u32[]{:S(2)}) copy-start(bf16[512,256]{0,1:T(8,128)(2,1)S(1)} %fusion.22) | copy-start | bytes 786436
  78.1 6.2 %copy-start.21 = (bf16[1024,256]{0,1:T(8,128)(2,1)}, bf16[1024,256]{0,1:T(8,128)(2,1)S(1)}, u32[]{:S(2)}) copy-start(bf16[1024,256]{0,1:T(8,128)(2,1)S(1)} %get-tuple-element.57) | copy-start | bytes 1572868
  91.7 9.5 %copy-start.60 = (bf16[2048,256]{1,0:T(8,128)(2,1)S(1)}, bf16[2048,256]{1,0:T(8,128)(2,1)}, u32[]{:S(2)}) copy-start(bf16[2048,256]{1,0:T(8,128)(2,1)} %param.47) | copy-start | bytes 3145732
  91.7 9.5 %copy-start.62 = (f32[256]{0:T(256)S(1)}, f32[256]{0:T(256)}, u32[]{:S(2)}) copy-start(f32[256]{0:T(256)} %param.48) | copy-start | bytes 3076
  115.0 7.3 %copy-start.22 = (bf16[1024,256]{0,1:T(8,128)(2,1)S(1)}, bf16[1024,256]{0,1:T(8,128)(2,1)}, u32[]{:S(2)}) copy-start(bf16[1024,256]{0,1:T(8,128)(2,1)} %copy-done.21) | copy-start | bytes 1572868
  136.1 12.8 %collective-permute-start.2 = (bf16[512,512]{0,1:T(8,128)(2,1)}, bf16[512,512]{0,1:T(8,128)(2,1)}, u32[]{:S(2)}, u32[]{:S(2)}) collective-permute-start(bf16[512,512]{0,1:T(8,128)(2,1)} %fusion.41), channel_id=1, source_target_pairs={{0,1},{1,0},{2,3},{3,2},{4,5},{5,4},{6,7},{7,6},{8,9},{9,8},{10,11... | collective-permute-start | bytes 1572872 | tf_op jit(solution)/shard_map/ppermute | solution.py:854
  138.2 5.9 %copy-start.40 = (f32[512]{0:T(512)S(1)}, f32[512]{0:T(512)}, u32[]{:S(2)}) copy-start(f32[512]{0:T(512)} %copy-done.39) | copy-start | bytes 6148
  141.8 8.4 %copy-start.32 = (bf16[256,256]{1,0:T(8,128)(2,1)S(1)}, bf16[256,256]{1,0:T(8,128)(2,1)}, u32[]{:S(2)}) copy-start(bf16[256,256]{1,0:T(8,128)(2,1)} %param.38) | copy-start | bytes 393220
  141.8 8.7 %copy-start.34 = (bf16[256,256]{1,0:T(8,128)(2,1)S(1)}, bf16[256,256]{1,0:T(8,128)(2,1)}, u32[]{:S(2)}) copy-start(bf16[256,256]{1,0:T(8,128)(2,1)} %param.39) | copy-start | bytes 393220
  144.1 6.7 %copy-start.20 = (bf16[512,512]{1,0:T(8,128)(2,1)S(1)}, bf16[512,512]{1,0:T(8,128)(2,1)}, u32[]{:S(2)}) copy-start(bf16[512,512]{1,0:T(8,128)(2,1)} %copy-done.19) | copy-start | bytes 1572868
  144.1 7.9 %copy-start.14 = (bf16[8,32,512]{2,1,0:T(8,128)(2,1)S(1)}, bf16[8,32,512]{2,1,0:T(8,128)(2,1)}, u32[]{:S(2)}) copy-start(bf16[8,32,512]{2,1,0:T(8,128)(2,1)} %get-tuple-element.98) | copy-start | bytes 786436
  145.5 8.3 %copy-start.6 = (f32[512,256]{1,0:T(8,128)S(1)}, f32[512,256]{1,0:T(8,128)}, u32[]{:S(2)}) copy-start(f32[512,256]{1,0:T(8,128)} %copy-done.5) | copy-start | bytes 1572868
  145.6 9.2 %copy-start.13 = (bf16[512,256]{1,0:T(8,128)(2,1)S(1)}, bf16[512,256]{1,0:T(8,128)(2,1)}, u32[]{:S(2)}) copy-start(bf16[512,256]{1,0:T(8,128)(2,1)} %copy-done.12) | copy-start | bytes 786436
  145.6 9.2 %copy-start.24 = (bf16[512,8,32]{0,2,1:T(8,128)(2,1)S(1)}, bf16[512,8,32]{0,2,1:T(8,128)(2,1)}, u32[]{:S(2)}) copy-start(bf16[512,8,32]{0,2,1:T(8,128)(2,1)} %copy-done.23) | copy-start | bytes 786436
  150.8 6.5 %copy-start.48 = (f32[256]{0:T(256)S(1)}, f32[256]{0:T(256)}, u32[]{:S(2)}) copy-start(f32[256]{0:T(256)} %convert_reduce_fusion.1) | copy-start | bytes 3076
  150.8 6.5 %copy-start.49 = (f32[256]{0:T(256)S(1)}, f32[256]{0:T(256)}, u32[]{:S(2)}) copy-start(f32[256]{0:T(256)} %get-tuple-element.33) | copy-start | bytes 3076
  150.8 6.5 %copy-start.50 = (f32[256]{0:T(256)S(1)}, f32[256]{0:T(256)}, u32[]{:S(2)}) copy-start(f32[256]{0:T(256)} %get-tuple-element.36) | copy-start | bytes 3076
  150.9 6.4 %copy-start.51 = (f32[256]{0:T(256)S(1)}, f32[256]{0:T(256)}, u32[]{:S(2)}) copy-start(f32[256]{0:T(256)} %get-tuple-element.38) | copy-start | bytes 3076
  150.9 6.4 %copy-start.52 = (f32[1,256]{1,0:T(1,128)S(1)}, f32[1,256]{1,0:T(1,128)}, u32[]{:S(2)}) copy-start(f32[1,256]{1,0:T(1,128)} %stack.20) | copy-start | bytes 3076
  150.9 6.4 %copy-start.57 = (f32[256]{0:T(256)S(1)}, f32[256]{0:T(256)}, u32[]{:S(2)}) copy-start(f32[256]{0:T(256)} %get-tuple-element.31) | copy-start | bytes 3076
  150.9 6.4 %copy-start.58 = (f32[256]{0:T(256)S(1)}, f32[256]{0:T(256)}, u32[]{:S(2)}) copy-start(f32[256]{0:T(256)} %get-tuple-element.35) | copy-start | bytes 3076
  (38 other events, 124.3 us)

commit v2 on v0

--- a/solution.py
+++ b/solution.py
@@ -1,8 +1,12 @@
+import functools
 import math
+from types import SimpleNamespace
 
 import jax
 import jax.numpy as jnp
 from jax import lax
+from jax.experimental import pallas as pl
+from jax.experimental.pallas import tpu as pltpu
 from jax.sharding import PartitionSpec as P
 
 HEADS = 8
@@ -347,9 +351,1208 @@
     return (encoded, features_grad, first_part, second_part) + tuple(dense)
 
 
+MESH = pl.DeviceIdType.MESH
+CORE, X, Y, Z0, Z1 = range(5)
+STEPS = {CORE: 1, Y: 2, Z0: 4, Z1: 8}
+PLANE, COLUMN = (X, Y), (Z0, Z1)
+DENSE = (
+    (64, ((CORE,), PLANE, COLUMN)),
+    (64, ((CORE,), PLANE, COLUMN)),
+    (64, ((CORE,), COLUMN, PLANE)),
+    (64, ((CORE,), PLANE, COLUMN)),
+    (64, ((CORE,), (X,), (Y,), COLUMN)),
+    (32, ((CORE,), (Y,), (X,), COLUMN)),
+)
+GRADS = (
+    ((Y,), (Z0,), (Z1,)),
+    ((Z0,), (Y,), (Z1,)),
+    ((Y,), (Z0,), (Z1,)),
+    ((Y,), (Z0,), (Z1,)),
+    ((Z0,), (Y,), (Z1,)),
+    ((Y,), (Z0,), (Z1,)),
+)
+ENDS, MIDDLE = 5, 6
+TAPS = 9
+LANES = 128
+WINDOW = 4.0
+DELAY = 2.0
+PROJECT, QUERY, VALUE, OUTPUT, FIRST_GAIN, FIRST_SHIFT, SHRINK, FINAL_GAIN, FINAL_SHIFT, EXPAND = range(10)
+
+
+def own_bits():
+    page, strip = lax.axis_index("page"), lax.axis_index("strip")
+    bits = {name: (page // step) % 2 for name, step in STEPS.items()}
+    bits[X] = strip
+    peers = {}
+    for names in ((CORE,), (X,), (Y,), (Z0,), (Z1,), COLUMN, PLANE, (CORE, X)):
+        there = page
+        for name in names:
+            if name != X:
+                there = there + STEPS[name] - 2 * STEPS[name] * bits[name]
+        peers[names] = (there, 1 - strip if X in names else strip)
+    return bits, peers
+
+
+def enter(peers):
+    barrier = pltpu.get_barrier_semaphore()
+    for peer in peers.values():
+        pl.semaphore_signal(barrier, inc=1, device_id=peer, device_id_type=MESH)
+    pl.semaphore_wait(barrier, len(peers))
+
+
+def remote(source, target, sends, recvs, peer):
+    return pltpu.make_async_remote_copy(
+        source, target, sends, recvs, device_id=peer, device_id_type=MESH
+    )
+
+
+def flat(order):
+    return [name for stage in order for name in stage]
+
+
+def slot_of(names, place):
+    slot = 0
+    for name in names:
+        slot = slot * 2 + place[name]
+    return slot
+
+
+class Reduction:
+    def __init__(self, order, group, bits, peers, current, parts, sends, recvs, back, keep):
+        self.order, self.bits, self.peers = order, bits, peers
+        self.current, self.parts = current, parts
+        self.sends, self.recvs = sends, recvs
+        self.whole = current if back else None
+        self.keep = keep
+        self.left = [group * 2 ** len(flat(order[step:])) for step in range(len(order) + 1)]
+        self.flights = None
+
+    def toward(self, names):
+        for code in range(1, 2 ** len(names)):
+            flips = [code >> number & 1 for number in range(len(names))]
+            key = tuple(name for name, flip in zip(names, flips) if flip)
+            place = {
+                name: 1 - self.bits[name] if flip else self.bits[name]
+                for name, flip in zip(names, flips)
+            }
+            yield code - 1, self.peers[key], slot_of(names, place)
+
+    def stage(self, step):
+        return self.order[min(step, 2 * len(self.order) - 1 - step)]
+
+    def begin(self, step):
+        count = len(self.order)
+        level = min(step, 2 * count - 1 - step)
+        names = self.stage(step)
+        size = self.left[level + 1]
+        self.flights = []
+        mark = sum(2 ** len(self.stage(before)) - 1 for before in range(step))
+        for number, peer, slot in self.toward(names):
+            if step < count:
+                source = self.current.at[pl.ds(slot * size, size)]
+                target = self.parts.at[pl.ds(self.left[0] - self.left[step] + number * size, size)]
+            else:
+                first = 0
+                for depth in range(level + 1):
+                    first += slot_of(self.order[depth], self.bits) * self.left[depth + 1]
+                source = target = self.whole.at[pl.ds(first, size)]
+            flight = remote(
+                source, target, self.sends.at[number], self.recvs.at[mark + number], peer
+            )
+            flight.start()
+            self.flights.append(flight)
+
+    def end(self, step):
+        count = len(self.order)
+        for flight in self.flights:
+            flight.wait()
+        if step >= count:
+            return
+        size = self.left[step + 1]
+        offset = self.left[0] - self.left[step]
+        total = self.current[pl.ds(slot_of(self.order[step], self.bits) * size, size)]
+        total = total.astype(jnp.float32)
+        for number in range(len(self.flights)):
+            total += self.parts[pl.ds(offset + number * size, size)].astype(jnp.float32)
+        total = total.astype(jnp.bfloat16)
+        if step == count - 1:
+            self.keep(total)
+            return
+        following = self.parts.at[pl.ds(offset, size)]
+        following[...] = total
+        self.current = following
+
+
+class Doubling:
+    def __init__(self, order, peers, sums, parts, sends, recvs):
+        self.order, self.peers = order, peers
+        self.sums, self.parts, self.sends, self.recvs = sums, parts, sends, recvs
+        self.flight = None
+
+    def begin(self, step):
+        self.flight = remote(
+            self.sums.at[step],
+            self.parts.at[step],
+            self.sends.at[step],
+            self.recvs.at[step],
+            self.peers[(self.order[step],)],
+        )
+        self.flight.start()
+
+    def end(self, step):
+        self.flight.wait()
+        self.sums[step + 1] = self.sums[step] + self.parts[step]
+
+
+def link_plan(units, window):
+    events = [(ready, 1, unit, 0) for unit, (ready, _) in enumerate(units)]
+    queue, busy, actions = [], {}, []
+    while events:
+        events.sort()
+        now, kind, unit, step = events.pop(0)
+        if kind == 0:
+            actions.append((now, False, unit, step))
+            step += 1
+        if step < len(units[unit][1]):
+            left = sum(max(cost.values()) + DELAY for cost in units[unit][1][step:])
+            queue.append((-left, unit, step))
+        queue.sort()
+        held, waiting = set(), []
+        for left, unit, step in queue:
+            cost = units[unit][1][step]
+            if any(link in held or busy.get(link, 0.0) - now >= window for link in cost):
+                held.update(cost)
+                waiting.append((left, unit, step))
+                continue
+            for link, spent in cost.items():
+                busy[link] = max(now, busy.get(link, 0.0)) + spent
+            actions.append((now, True, unit, step))
+            events.append((max(busy[link] for link in cost) + DELAY, 0, unit, step))
+        queue = waiting
+    return actions
+
+
+def link_costs(order, size, back):
+    costs = []
+    for names in order:
+        size = size / 2 ** len(names)
+        per_flow = size / 9e4
+        if names == (CORE,):
+            costs.append({CORE: size / 6e5})
+        elif names == PLANE:
+            costs.append({X: 4 * per_flow, Y: 4 * per_flow})
+        elif names == COLUMN:
+            costs.append({MIDDLE: 8 * per_flow, ENDS: 6 * per_flow})
+        elif names == (Z0,):
+            costs.append({ENDS: 2 * per_flow})
+        elif names == (Z1,):
+            costs.append({MIDDLE: 4 * per_flow, ENDS: 2 * per_flow})
+        else:
+            costs.append({names[0]: 2 * per_flow})
+    return costs + costs[::-1] if back else costs
+
+
+def shifted(value):
+    side = value.shape[0]
+    wide = value.astype(jnp.float32)
+    column = lax.broadcasted_iota(jnp.int32, wide.shape, 0)
+    later = jnp.where(column < side - 1, pltpu.roll(wide, side - 1, 0), 0.0)
+    earlier = jnp.where(column > 0, pltpu.roll(wide, 1, 0), 0.0)
+    return later.astype(jnp.bfloat16), earlier.astype(jnp.bfloat16)
+
+
+def gelu_both(value):
+    bell = 0.5 * (1.0 + lax.erf(value * math.sqrt(0.5)))
+    density = jnp.exp(-0.5 * value * value) * (1.0 / math.sqrt(2.0 * math.pi))
+    return value * bell, bell + value * density
+
+
+def dot(left, right):
+    return jnp.dot(left, right, preferred_element_type=jnp.float32)
+
+
+def dot_nt(left, right):
+    return lax.dot_general(
+        left, right, (((1,), (1,)), ((), ())), preferred_element_type=jnp.float32
+    )
+
+
+def low(value):
+    return value.astype(jnp.bfloat16)
+
+
+def row_sum(value):
+    return jnp.sum(value.astype(jnp.float32), axis=0, keepdims=True)
+
+
+def norm_parts(value):
+    center = value - jnp.mean(value, axis=-1, keepdims=True)
+    spread = jnp.mean(center * center, axis=-1, keepdims=True)
+    root = lax.rsqrt(spread + 1e-05)
+    return center * root, root
+
+
+def norm_back(normal, root, gain, upstream):
+    weighted = upstream * gain
+    return root * (
+        weighted
+        - jnp.mean(weighted, axis=-1, keepdims=True)
+        - normal * jnp.mean(weighted * normal, axis=-1, keepdims=True)
+    )
+
+
+def page_kernel(side, names, *refs):
+    r = SimpleNamespace(**dict(zip(names, refs)))
+    width = r.w_project.shape[1]
+    feat_ext = r.feat_ext
+    edge = 2 * side
+    length = feat_ext.shape[0] - 2 * edge
+    feat = feat_ext.at[pl.ds(edge, length)]
+    f32, bf16 = jnp.float32, jnp.bfloat16
+    r.loads = (
+        (r.features, feat),
+        (r.first_kernel, r.w_first),
+        (r.frozen_scale, r.v_scale),
+        (r.frozen_shift, r.v_shift),
+        (r.second_kernel, r.w_second),
+        (r.project_weight, r.w_project),
+        (r.project_bias, r.v_project),
+        (r.query_weight, r.w_query),
+        (r.key_weight, r.w_key),
+        (r.value_weight, r.w_value),
+        (r.query_bias, r.v_query),
+        (r.value_bias, r.v_value),
+        (r.output_weight, r.w_output),
+        (r.expand_weight, r.w_expand),
+        (r.shrink_weight, r.w_shrink),
+        (r.cotangent, r.cot),
+        (r.output_bias, r.v_output),
+        (r.first_gain, r.v_first_gain),
+        (r.first_shift, r.v_first_shift),
+        (r.expand_bias, r.v_expand),
+        (r.shrink_bias, r.v_shrink),
+        (r.final_gain, r.v_final_gain),
+        (r.final_shift, r.v_final_shift),
+    )
+    channels = feat_ext.shape[1]
+    hidden_units = r.w_expand.shape[1]
+    head_size = width // HEADS
+    rows = length // side
+    factor = head_size ** (-0.5)
+    bits, peers = own_bits()
+    strip, core = bits[X], bits[CORE]
+    clock = [0.0]
+
+    loads = {}
+    for number, (source, target) in enumerate(r.loads):
+        pieces = source.shape[0] if len(source.shape) == 3 else 1
+        semaphore = r.load_sems.at[number]
+        for piece in range(pieces):
+            at = pl.ds(piece, 1) if pieces > 1 else pl.ds(0, source.shape[0])
+            pltpu.make_async_copy(source.at[at], target.at[at], semaphore).start()
+        loads[number] = pltpu.make_async_copy(source, target, semaphore)
+    enter(peers)
+
+    exchanged = [0]
+
+    def exchange(source, target, peer):
+        number = exchanged[0]
+        exchanged[0] += 1
+        copy = remote(source, target, r.pair_sends.at[number], r.pair_recvs.at[number], peer)
+        copy.start()
+        return copy
+
+    def aligned(start, size, unit=side):
+        return pl.ds(pl.multiple_of(start, unit), size)
+
+    own_edge = (1 - strip) * (length - edge)
+    feat_halo = exchange(
+        r.features.at[aligned(own_edge, edge)],
+        r.feat_ext.at[aligned(strip * (length + edge), edge)],
+        peers[(X,)],
+    )
+
+    turn, height, breadth = r.quarter_turns[0], r.heights[0], r.widths[0]
+    odd = turn % 2
+    lane = lax.broadcasted_iota(jnp.int32, (side, LANES), 1)
+    count = lax.broadcasted_iota(jnp.int32, (side, LANES), 0)
+    inverse = jnp.exp((lane // 2).astype(f32) * (-2.0 * math.log(10000.0) / LANES))
+    row_place = strip * rows + count
+    row_place = jnp.where(row_place >= side, row_place - side, row_place)
+    row_flip = ((turn == 1) | (turn == 2)).astype(jnp.int32)
+    column_flip = (turn // 2) % 2
+    for place, flip, extent, first, table, bias in (
+        (
+            row_place,
+            row_flip,
+            height + odd * (breadth - height),
+            1 - odd,
+            r.table_row,
+            r.bias_row,
+        ),
+        (
+            count,
+            column_flip,
+            breadth + odd * (height - breadth),
+            odd,
+            r.table_col,
+            r.bias_col,
+        ),
+    ):
+        place = place + flip * (side - 1 - 2 * place)
+        along = (place + 1).astype(f32) / (jnp.full((side, LANES), extent).astype(f32) + 1e-06)
+        phase = along * (2.0 * math.pi) * inverse
+        sines = jnp.where(lane % 2 == 0, jnp.sin(phase), jnp.cos(phase))
+        share = jnp.full((side, LANES), first).astype(f32)
+        table[:, pl.ds(0, LANES)] = sines * share
+        table[:, pl.ds(LANES, LANES)] = sines * (1.0 - share)
+        bias[...] = jnp.where(place < extent, 0.0, -10000.0)
+
+    pool, dense, owned = r.pool, r.dense, r.owned
+    dense_units = len(DENSE)
+    reducers, costs = [], []
+    ready_dense = [30.0, 30.2, 30.4, 30.6, 43.0, 44.0]
+    unit_slots = 24
+    begin, marks = 0, 0
+    for unit, (slots, order) in enumerate(DENSE):
+        group = slots // 32
+
+        def keep_dense(value, begin=begin, group=group, order=order):
+            dense[pl.ds(begin + slot_of(flat(order), bits) * group, group)] = value
+
+        reducers.append(
+            Reduction(
+                order,
+                group,
+                bits,
+                peers,
+                dense.at[pl.ds(begin, slots)],
+                r.dense_parts.at[pl.ds(begin, slots)],
+                r.dense_sends.at[pl.ds(3 * unit, 3)],
+                r.dense_recvs.at[pl.ds(14 * unit, 14)],
+                True,
+                keep_dense,
+            )
+        )
+        costs.append((ready_dense[unit], link_costs(order, slots * 8192, True)))
+        begin += slots
+    for unit, order in enumerate(GRADS):
+
+        def keep_grad(value, unit=unit):
+            half = value.shape[1] // 2
+            for across in range(3):
+                tap = unit % 3 * 3 + across
+                owned[unit // 3, 0, tap] = value[across, :half]
+                owned[unit // 3, 1, tap] = value[across, half:]
+
+        reducers.append(
+            Reduction(
+                order,
+                3,
+                bits,
+                peers,
+                pool.at[pl.ds(unit * unit_slots, unit_slots)],
+                r.parts.at[unit],
+                r.grad_sends.at[pl.ds(unit, 1)],
+                r.grad_recvs.at[pl.ds(3 * unit, 3)],
+                False,
+                keep_grad,
+            )
+        )
+        made = 53.0 + unit if unit < 3 else 61.0 + unit - 3
+        costs.append((made, link_costs(order, 393216, False)))
+    small_order = (CORE, X, Y, Z0, Z1)
+    small = r.small_sums
+    reducers.append(
+        Doubling(
+            small_order, peers, small, r.small_parts, r.small_sends, r.small_recvs
+        )
+    )
+    costs.append((44.0, [{CORE: 0.2}, {X: 0.5}, {Y: 0.5}, {ENDS: 0.5}, {MIDDLE: 1.0, ENDS: 0.5}]))
+    agenda = link_plan(costs, WINDOW)
+
+    def work(spent):
+        clock[0] += spent
+        while agenda and agenda[0][0] <= clock[0]:
+            _, begins, unit, step = agenda.pop(0)
+            if begins:
+                reducers[unit].begin(step)
+            else:
+                reducers[unit].end(step)
+
+    stores = []
+
+    def store(source, target):
+        stores.append(pltpu.make_async_copy(source, target, r.out_sems.at[len(stores)]))
+        stores[-1].start()
+
+    def settle(at):
+        clock[0] = at
+        work(0.0)
+
+    def spread(source, target, first, count):
+        def one(row, carry):
+            at = aligned(row * side, side)
+            value = source[at]
+            later, earlier = shifted(value)
+            target[0, at] = later
+            target[1, at] = value
+            target[2, at] = earlier
+            return carry
+
+        lax.fori_loop(first, first + count, one, 0)
+
+    def conv(x3, weight, start, count, transposed):
+        total = None
+        for tap in range(TAPS):
+            down, across = tap // 3, tap % 3
+            if transposed:
+                window = pl.ds(start + side * (2 - down), count)
+                term = dot_nt(x3[across, window], weight[tap])
+            else:
+                window = pl.ds(start + side * down, count)
+                term = dot(x3[2 - across, window], weight[tap])
+            total = term if total is None else total + term
+        return total
+
+    x3 = r.x3
+    scale, shift = r.v_scale, r.v_shift
+
+    def vector(ref, piece=0):
+        return ref[pl.ds(piece * width, width)].reshape(1, width)
+
+
+    loads[0].wait()
+    feat_ext[aligned(strip * (length + edge), edge)] = jnp.zeros((edge, channels), bf16)
+    spread(feat_ext, x3, 2, rows)
+    own_lanes = aligned(strip * length, length, length)
+    other_lanes = aligned((1 - strip) * length, length, length)
+
+    def share(every, lanes, source_page, target_page, peer):
+        return exchange(every.at[source_page, :, lanes], every.at[target_page, :, lanes], peer)
+
+    r.features_all[0, :, own_lanes] = feat[...].T
+    feat_copies = [
+        share(r.features_all, own_lanes, 0, 0, peers[(X,)]),
+        share(r.features_all, own_lanes, 0, 1, peers[(CORE,)]),
+    ]
+    for number in (1, 2, 3):
+        loads[number].wait()
+    feat_halo.wait()
+    spread(feat_ext, x3, 0, 2)
+    spread(feat_ext, x3, rows + 2, 2)
+    hidden = r.hidden
+    half_rows = (length + edge) // 2
+    for part in range(2):
+        at = pl.ds(part * half_rows, half_rows)
+        pre = conv(x3, r.w_first, part * half_rows, half_rows, False)
+        value, slope = gelu_both(pre * scale[0:1] + shift[0:1])
+        hidden[at] = low(value)
+        r.slope_first[at] = slope * scale[0:1]
+    for begin, inside in ((0, strip), (length + side, 1 - strip)):
+        at = pl.ds(begin, side)
+        keep = jnp.broadcast_to(inside, (side, channels)).astype(f32)
+        hidden[at] = low(hidden[at].astype(f32) * keep)
+        r.slope_first[at] = r.slope_first[at] * keep
+    spread(hidden, x3, 0, rows + 2)
+    r.hidden_all[0, :, own_lanes] = hidden[pl.ds(side, length)].T
+
+    for number in (4, 5, 6):
+        loads[number].wait()
+    block, source, plain = r.block, r.source, r.plain
+    half = length // 2
+    plain_copies = []
+    for part in range(2):
+        at = pl.ds(part * half, half)
+        pre = conv(x3, r.w_second, part * half, half, False)
+        value, slope = gelu_both(pre * scale[1:2] + shift[1:2] + feat[at].astype(f32))
+        block[at] = low(value)
+        r.direct[at] = slope
+        rows_here = dot(block[at], r.w_project[...]) + vector(r.v_project)
+        source[at] = rows_here
+        plain[at] = low(rows_here)
+        plain_copies.append(
+            exchange(plain.at[at], plain.at[pl.ds(length + part * half, half)], peers[(X,)])
+        )
+    for number in range(7, 12):
+        loads[number].wait()
+
+    joint, keys, values = r.joint, r.keys, r.values
+    keys_t, values_t = r.keys_t, r.values_t
+    table_row, table_col = r.table_row, r.table_col
+    bias_row, bias_col = r.bias_row, r.bias_col
+
+    def keys_of(which):
+        base = which * length
+        for row in range(rows):
+            at = pl.ds(base + row * side, side)
+            index = which * rows + row
+            position = table_row[index : index + 1] + table_col[...]
+            rows_here = source[pl.ds(row * side, side)] if which == 0 else plain[at].astype(f32)
+            joint[at] = low(rows_here + position)
+            r.bias[at] = jnp.minimum(bias_row[index : index + 1], bias_col[...])
+        at = pl.ds(base, length)
+        keys[at] = low(dot(joint[at], r.w_key[...]))
+        values[at] = low(dot(plain[at], r.w_value[...]) + vector(r.v_value))
+        keys_t[which] = keys[at].T
+        values_t[which] = values[at].T
+
+    lane_head = lax.broadcasted_iota(jnp.int32, (1, width), 1) // head_size
+
+    def only(head, value):
+        return jnp.where(lane_head == head, value, 0).astype(bf16)
+
+    quarter = length // LANES
+    tile = length // 64
+
+    def pool_at(which, head, lane):
+        return pl.ds(((which * HEADS + head) * quarter + lane) * tile, tile)
+
+    keys_of(0)
+    queries = r.queries
+    queries[...] = low(dot(joint[pl.ds(0, length)], r.w_query[...]) + vector(r.v_query))
+    stat, mixed_parts = r.stat, r.mixed_parts
+
+    def attend(which):
+        def one(head, carry):
+            at = pl.ds(which * length, length)
+            scores = dot_nt(keys[at], only(head, queries[...])) * factor
+            bias = r.bias[at]
+            scores = scores + jnp.concatenate([bias] * quarter, axis=1)
+            peak = jnp.max(scores, axis=0, keepdims=True)
+            powers = jnp.exp(scores - peak)
+            stat[head, 2 * which : 2 * which + 1] = peak
+            stat[head, 2 * which + 1 : 2 * which + 2] = jnp.sum(powers, axis=0, keepdims=True)
+            powers = low(powers)
+            for lane in range(quarter):
+                pool[pool_at(which, head, lane)] = powers[
+                    :, lane * LANES : (lane + 1) * LANES
+                ].reshape(tile, 64, LANES)
+            channel = aligned(head * head_size, head_size, head_size)
+            mixed_parts[which, channel] = dot(values_t[which, channel], powers)
+            return carry
+
+        lax.fori_loop(0, HEADS, one, 0)
+
+    attend(0)
+    for copy in plain_copies + feat_copies:
+        copy.wait()
+    hidden_copies = [
+        share(r.hidden_all, own_lanes, 0, 0, peers[(X,)]),
+        share(r.hidden_all, own_lanes, 0, 1, peers[(CORE,)]),
+    ]
+    feat_relay = share(r.features_all, other_lanes, 0, 1, peers[(CORE,)])
+    keys_of(1)
+    attend(1)
+
+    shares_t = r.shares_t
+    for head in range(HEADS):
+        channel = pl.ds(head * head_size, head_size)
+        first_peak, first_sum = stat[head, 0:1], stat[head, 1:2]
+        second_peak, second_sum = stat[head, 2:3], stat[head, 3:4]
+        peak = jnp.maximum(first_peak, second_peak)
+        first_scale, second_scale = jnp.exp(first_peak - peak), jnp.exp(second_peak - peak)
+        total = first_scale * first_sum + second_scale * second_sum
+        first_scale, second_scale = first_scale / total, second_scale / total
+        stat[head, 4:5] = first_scale
+        stat[head, 5:6] = second_scale
+        shares_t[0, channel] = jnp.broadcast_to(first_scale, (head_size, length))
+        shares_t[1, channel] = jnp.broadcast_to(second_scale, (head_size, length))
+    mixed = (shares_t[0] * mixed_parts[0] + shares_t[1] * mixed_parts[1]).T
+    combined = r.combined
+    combined[...] = low(mixed)
+
+    for number in range(12, len(loads)):
+        loads[number].wait()
+    small[...] = jnp.zeros_like(small)
+    activated, d_expanded = r.activated, r.d_expanded
+    ff_in, d_shrunk, d_attended, d_first = r.ff_in, r.d_shrunk, r.d_attended, source
+    d_combined = r.d_combined
+    chunk = 256
+    pieces = hidden_units // width
+
+    def tokens(step, carry):
+        at = aligned(step * chunk, chunk, chunk)
+        first_total = source[at] + dot(combined[at], r.w_output[...]) + vector(r.v_output)
+        first_normal, first_root = norm_parts(first_total)
+        normed = first_normal * vector(r.v_first_gain) + vector(r.v_first_shift)
+        ff = low(normed)
+        ff_in[at] = ff
+        slopes = []
+        shrunk = None
+        for piece in range(pieces):
+            lane = pl.ds(piece * width, width)
+            expanded = dot(ff, r.w_expand[:, lane]) + vector(r.v_expand, piece)
+            value, slope = gelu_both(expanded)
+            value = low(value)
+            activated[at, lane] = value
+            slopes.append(slope)
+            term = dot(value, r.w_shrink[lane])
+            shrunk = term if shrunk is None else shrunk + term
+        second_total = normed + shrunk + vector(r.v_shrink)
+        second_normal, second_root = norm_parts(second_total)
+        r.encoded_here[at] = low(
+            second_normal * vector(r.v_final_gain) + vector(r.v_final_shift)
+        )
+        upstream = r.cot[at].astype(f32)
+        small[0, FINAL_GAIN : FINAL_GAIN + 1] += row_sum(upstream * second_normal)
+        small[0, FINAL_SHIFT : FINAL_SHIFT + 1] += row_sum(upstream)
+        d_second = norm_back(second_normal, second_root, vector(r.v_final_gain), upstream)
+        d_low = low(d_second)
+        d_shrunk[at] = d_low
+        small[0, SHRINK : SHRINK + 1] += row_sum(d_low)
+        d_normed = d_second
+        for piece in range(pieces):
+            lane = pl.ds(piece * width, width)
+            d_piece = low(dot_nt(d_low, r.w_shrink[lane]) * slopes[piece])
+            d_expanded[at, lane] = d_piece
+            small[0, EXPAND + piece : EXPAND + piece + 1] += row_sum(d_piece)
+            d_normed = d_normed + dot_nt(d_piece, r.w_expand[:, lane])
+        small[0, FIRST_GAIN : FIRST_GAIN + 1] += row_sum(d_normed * first_normal)
+        small[0, FIRST_SHIFT : FIRST_SHIFT + 1] += row_sum(d_normed)
+        d_total = norm_back(first_normal, first_root, vector(r.v_first_gain), d_normed)
+        d_first[at] = d_total
+        d_low = low(d_total)
+        d_attended[at] = d_low
+        small[0, OUTPUT : OUTPUT + 1] += row_sum(d_low)
+        d_combined[at] = low(dot_nt(d_low, r.w_output[...]))
+        return carry
+
+    lax.fori_loop(0, length // chunk, tokens, 0)
+
+    store(r.encoded_here, r.encoded)
+
+    def put(unit, value):
+        dense[pl.ds(unit * 32, 32)] = low(value).reshape(32, 16, width)
+
+    for part in range(hidden_units // 512):
+        lane = pl.ds(part * 512, 512)
+        put(part, dot(activated[:, lane].T, d_shrunk[...]))
+    ff_t = ff_in[...].T
+    for part in range(pieces // 2):
+        both = dot(ff_t, d_expanded[:, pl.ds(part * 512, 512)])
+        put(4 + part, jnp.concatenate([both[:, :width], both[:, width:]], axis=0))
+    settle(30.0)
+
+    deltas = r.deltas
+    d_scaled = r.d_scaled
+    total = None
+    for which in range(2):
+        scaled = low(d_combined[...].astype(f32) * shares_t[which].T)
+        d_scaled[which] = scaled
+        term = scaled.T.astype(f32) * mixed_parts[which]
+        total = term if total is None else total + term
+    for head in range(HEADS):
+        delta = jnp.sum(total[head * head_size : (head + 1) * head_size], axis=0, keepdims=True)
+        deltas[head, 0:1] = delta * stat[head, 4:5]
+        deltas[head, 1:2] = delta * stat[head, 5:6]
+    work(0.5)
+    d_queries_t = r.d_queries_t
+    d_queries_t[...] = jnp.zeros_like(d_queries_t)
+    spare_query, spare_scaled = activated, d_expanded
+    for head in range(HEADS):
+        spare_query[:, pl.ds(head * width, width)] = only(head, queries[...])
+
+    def stacked(which):
+        return jnp.concatenate(
+            [
+                pool[pool_at(which, head, lane)].reshape(length, LANES)
+                for head in range(HEADS)
+                for lane in range(quarter)
+            ],
+            axis=1,
+        )
+
+    def heads_down(wide):
+        return jnp.concatenate(
+            [wide[:, pl.ds(head * width, width)] for head in range(HEADS)], axis=0
+        )
+
+    def attend_back(which):
+        at = pl.ds(which * length, length)
+        for head in range(HEADS):
+            spare_scaled[:, pl.ds(head * width, width)] = only(head, d_scaled[which])
+        d_values = low(dot(stacked(which), heads_down(spare_scaled)))
+        work(1.2)
+        for head in range(HEADS):
+            d_prob = dot_nt(values[at], spare_scaled[:, pl.ds(head * width, width)])
+            d_prob = d_prob - deltas[head, which : which + 1]
+            pieces_here = []
+            for lane in range(quarter):
+                powers = pool[pool_at(which, head, lane)].reshape(length, LANES).astype(f32)
+                d_tile = low(powers * d_prob[:, lane * LANES : (lane + 1) * LANES])
+                pool[pool_at(which, head, lane)] = d_tile.reshape(tile, 64, LANES)
+                pieces_here.append(d_tile)
+            channel = pl.ds(head * head_size, head_size)
+            d_queries_t[channel] += dot(
+                keys_t[which, channel], jnp.concatenate(pieces_here, axis=1)
+            )
+            work(0.3)
+        d_keys = low(dot(stacked(which), heads_down(spare_query)) * factor)
+        work(1.2)
+        d_rows = dot_nt(d_keys, r.w_key[...]) + dot_nt(d_values, r.w_value[...])
+        small[0, VALUE : VALUE + 1] += row_sum(d_values)
+        return (
+            d_rows,
+            dot(joint[at].T, d_keys),
+            dot(plain[at].T, d_values),
+        )
+
+    d_other, key_grad, value_grad = attend_back(1)
+    d_combined[...] = low(d_other)
+    d_rows_copy = exchange(d_combined, r.d_rows_in, peers[(X,)])
+    work(0.3)
+    d_own, more_key, more_value = attend_back(0)
+    d_queries = low(d_queries_t[...].T * factor)
+    small[0, QUERY : QUERY + 1] = row_sum(d_queries)
+    joint_t = joint[pl.ds(0, length)].T
+    put(
+        8,
+        jnp.concatenate([dot(joint_t, d_queries), key_grad + more_key], axis=0),
+    )
+    put(
+        9,
+        jnp.concatenate([value_grad + more_value, dot(combined[...].T, d_attended[...])], axis=0),
+    )
+    settle(43.0)
+    d_source = d_first[...] + dot_nt(d_queries, r.w_query[...]) + d_own
+    d_rows_copy.wait()
+    d_source = low(d_source + r.d_rows_in[...].astype(f32))
+    small[0, PROJECT : PROJECT + 1] = row_sum(d_source)
+    direct = r.direct
+    late_ext = r.late_ext
+    late = late_ext.at[pl.ds(edge, length)]
+    direct[...] = dot_nt(d_source, r.w_project[...]) * r.direct[...]
+    late[...] = low(direct[...] * scale[1:2])
+
+    blank = jnp.zeros((edge, channels), bf16)
+    halo = exchange(
+        late_ext.at[aligned(edge + own_edge, edge)],
+        late_ext.at[aligned(strip * (length + edge), edge)],
+        peers[(X,)],
+    )
+
+    def spread_out(source, first, target):
+        copies = []
+        there = aligned(side + strip * length, length)
+        for peer, page, strip_there, core_there in (
+            ((X,), 0, 1 - strip, core),
+            ((CORE, X), 1, 1 - strip, 1 - core),
+            ((CORE,), 1, strip, 1 - core),
+        ):
+            lane_here = aligned(strip_there * 2 * LANES + core_there * LANES, LANES, LANES)
+            copies.append(
+                exchange(
+                    source.at[pl.ds(first, length), lane_here], target.at[page, there], peers[peer]
+                )
+            )
+        lane_here = aligned(strip * 2 * LANES + core * LANES, LANES, LANES)
+        target[0, there] = source[pl.ds(first, length), lane_here]
+        for page in range(2):
+            target[page, pl.ds(0, side)] = blank[:side, :LANES]
+            target[page, pl.ds(side + 2 * length, side)] = blank[:side, :LANES]
+        return copies
+
+    late_copies = spread_out(late_ext, edge, r.late_page)
+    late_ext[aligned(strip * (length + edge), edge)] = blank
+    spread(late_ext, x3, 2, rows)
+    put(10, dot(block[...].T, d_source))
+    settle(44.0)
+    for copy in hidden_copies:
+        copy.wait()
+    hidden_relay = share(r.hidden_all, other_lanes, 0, 1, peers[(CORE,)])
+    halo.wait()
+    spread(late_ext, x3, 0, 2)
+    spread(late_ext, x3, rows + 2, 2)
+    early = hidden
+    for part in range(2):
+        at = pl.ds(part * half_rows, half_rows)
+        d_hidden = conv(x3, r.w_second, part * half_rows, half_rows, True)
+        early[at] = low(d_hidden * r.slope_first[at])
+        work(1.5)
+    early_copies = spread_out(early, side, r.early_page)
+    page3 = r.page3
+
+    def spread_pages(source):
+        def one(row, carry):
+            at = aligned(row * side, side)
+            for page in range(2):
+                value = source[page, at]
+                later, earlier = shifted(value)
+                page3[page, 0, at] = later
+                page3[page, 1, at] = value
+                page3[page, 2, at] = earlier
+            return carry
+
+        lax.fori_loop(0, 2 * rows + 2, one, 0)
+
+    def kernel_grads(left, first_unit):
+        for down in range(3):
+            window = pl.ds(side * (2 - down), 2 * length)
+            product = None
+            for page in range(2):
+                right = jnp.concatenate([page3[page, across, window] for across in range(3)], axis=1)
+                term = dot(left[page], right)
+                product = term if product is None else product + term
+            product = low(product)
+            unit = first_unit + down
+            order = reducers[dense_units + unit].order
+            size = product.shape[0] // 8
+            for chip in range(8):
+                place = {Y: chip % 2, Z0: chip // 2 % 2, Z1: chip // 4}
+                for across in range(3):
+                    pool[unit * unit_slots + slot_of(flat(order), place) * 3 + across] = product[
+                        chip * size : (chip + 1) * size, across * LANES : (across + 1) * LANES
+                    ]
+            work(1.0)
+
+    for copy in late_copies + [hidden_relay, feat_relay]:
+        copy.wait()
+    spread_pages(r.late_page)
+    settle(52.0)
+    kernel_grads(r.hidden_all, 0)
+    spread(early, x3, 0, rows + 2)
+    for part in range(2):
+        at = pl.ds(part * half, half)
+        direct[at] = conv(x3, r.w_first, part * half, half, True) + direct[at]
+        work(1.3)
+    store(direct, r.features_grad)
+    for copy in early_copies:
+        copy.wait()
+    spread_pages(r.early_page)
+    settle(60.0)
+    kernel_grads(r.features_all, 3)
+    settle(1e9)
+    store(small.at[5], r.small_out)
+    store(dense, r.dense_out)
+    finals = []
+    for which, here, out in (
+        (1, r.first_here, r.first_grad),
+        (0, r.second_here, r.second_grad),
+    ):
+        copy = exchange(owned.at[which, 1 - core], r.owned_sib.at[which], peers[(CORE,)])
+        finals.append((copy, which, here, out))
+    for copy, which, here, out in finals:
+        copy.wait()
+        here[:, :, aligned(core * LANES, LANES, LANES)] = owned[which, core].astype(f32)
+        here[:, :, aligned((1 - core) * LANES, LANES, LANES)] = r.owned_sib[which].astype(f32)
+        store(here, out)
+    for copy in stores:
+        copy.wait()
+
+
+def page_call(side, inputs):
+    f32, bf16 = jnp.float32, jnp.bfloat16
+    length, channels = inputs["features"].shape
+    width = inputs["project_weight"].shape[1]
+    hidden_units = inputs["expand_weight"].shape[1]
+    edge = 2 * side
+    dense_shape = ((2 * hidden_units + channels + 4 * width) // 16, 16, width)
+    hbm = pl.BlockSpec(memory_space=pl.ANY)
+    sems = pltpu.SemaphoreType.DMA
+    def place(array):
+        return smem if array.dtype == jnp.int32 else hbm
+
+    smem = pl.BlockSpec(memory_space=pltpu.SMEM)
+    outs = dict(
+        encoded=((length, width), bf16),
+        features_grad=((length, channels), f32),
+        first_grad=((TAPS, channels // 16, channels // 2), f32),
+        second_grad=((TAPS, channels // 16, channels // 2), f32),
+        dense_out=(dense_shape, bf16),
+        small_out=((24, width), f32),
+    )
+    scratch = dict(
+        w_first=((TAPS, channels, channels), bf16),
+        w_second=((TAPS, channels, channels), bf16),
+        w_project=((channels, width), bf16),
+        w_query=((width, width), bf16),
+        w_key=((width, width), bf16),
+        w_value=((width, width), bf16),
+        w_output=((width, width), bf16),
+        w_expand=((width, hidden_units), bf16),
+        w_shrink=((hidden_units, width), bf16),
+        cot=((length, width), bf16),
+        v_scale=(inputs["frozen_scale"].shape, f32),
+        v_shift=(inputs["frozen_shift"].shape, f32),
+        v_project=((width,), f32),
+        v_query=((width,), f32),
+        v_value=((width,), f32),
+        v_output=((width,), f32),
+        v_first_gain=((width,), f32),
+        v_first_shift=((width,), f32),
+        v_expand=((hidden_units,), f32),
+        v_shrink=((width,), f32),
+        v_final_gain=((width,), f32),
+        v_final_shift=((width,), f32),
+        encoded_here=((length, width), bf16),
+        direct=((length, channels), f32),
+        first_here=((TAPS, channels // 16, channels // 2), f32),
+        second_here=((TAPS, channels // 16, channels // 2), f32),
+        table_row=((side, width), f32),
+        table_col=((side, width), f32),
+        bias_row=((side, LANES), f32),
+        bias_col=((side, LANES), f32),
+        feat_ext=((length + 2 * edge, channels), bf16),
+        x3=((3, length + 2 * edge, channels), bf16),
+        hidden=((length + edge, channels), bf16),
+        slope_first=((length + edge, channels), f32),
+        features_all=((2, channels, 2 * length), bf16),
+        hidden_all=((2, channels, 2 * length), bf16),
+        block=((length, channels), bf16),
+        source=((length, width), f32),
+        plain=((2 * length, width), bf16),
+        joint=((2 * length, width), bf16),
+        bias=((2 * length, LANES), f32),
+        keys=((2 * length, width), bf16),
+        values=((2 * length, width), bf16),
+        keys_t=((2, width, length), bf16),
+        values_t=((2, width, length), bf16),
+        queries=((length, width), bf16),
+        stat=((HEADS, 8, length), f32),
+        deltas=((HEADS, 8, length), f32),
+        mixed_parts=((2, width, length), f32),
+        shares_t=((2, width, length), f32),
+        combined=((length, width), bf16),
+        activated=((length, hidden_units), bf16),
+        d_expanded=((length, hidden_units), bf16),
+        ff_in=((length, width), bf16),
+        d_shrunk=((length, width), bf16),
+        d_attended=((length, width), bf16),
+        d_combined=((length, width), bf16),
+        d_scaled=((2, length, width), bf16),
+        d_queries_t=((width, length), f32),
+        d_rows_in=((length, width), bf16),
+        late_ext=((length + 2 * edge, channels), bf16),
+        late_page=((2, 2 * length + edge, LANES), bf16),
+        early_page=((2, 2 * length + edge, LANES), bf16),
+        page3=((2, 3, 2 * length + edge, LANES), bf16),
+        pool=((2 * HEADS * (length // LANES) * (length // 64), 64, LANES), bf16),
+        parts=((6, 21, 64, LANES), bf16),
+        dense=(dense_shape, bf16),
+        dense_parts=(dense_shape, bf16),
+        small_sums=((6, 24, width), f32),
+        small_parts=((5, 24, width), f32),
+        owned=((2, 2, TAPS, channels // 16, LANES), bf16),
+        owned_sib=((2, TAPS, channels // 16, LANES), bf16),
+    )
+    sem_shapes = dict(
+        load_sems=(23,),
+        out_sems=(6,),
+        pair_sends=(20,),
+        pair_recvs=(20,),
+        grad_sends=(6,),
+        grad_recvs=(18,),
+        dense_sends=(3 * len(DENSE),),
+        dense_recvs=(14 * len(DENSE),),
+        small_sends=(5,),
+        small_recvs=(5,),
+    )
+    names = list(inputs) + list(outs) + list(scratch) + list(sem_shapes)
+    results = pl.pallas_call(
+        functools.partial(page_kernel, side, names),
+        out_shape=tuple(jax.ShapeDtypeStruct(*spec) for spec in outs.values()),
+        in_specs=[place(array) for array in inputs.values()],
+        out_specs=tuple([hbm] * len(outs)),
+        scratch_shapes=[pltpu.VMEM(*spec) for spec in scratch.values()]
+        + [sems(shape) for shape in sem_shapes.values()],
+        compiler_params=pltpu.CompilerParams(
+            collective_id=0, has_side_effects=True, vmem_limit_bytes=63 * 1024 * 1024
+        ),
+        name="page_step",
+    )(*inputs.values())
+    return SimpleNamespace(**dict(zip(outs, results)))
+
+
+def unpack_kernel(passed, dense_hbm, small_hbm, *refs):
+    f32 = jnp.float32
+    through, refs = refs[:passed], refs[passed:]
+    through_out, refs = refs[:passed], refs[passed:]
+    held, refs = refs[len(refs) - passed :], refs[: len(refs) - passed]
+    outs, (dense, wide, small, vector, vector_wide, in_sems, out_sems) = refs[:-7], refs[-7:]
+    project, project_b, query, query_b, key, value, value_b, output, output_b = outs[:9]
+    first_gain, first_shift, expand, expand_b, shrink, shrink_b, final_gain, final_shift = outs[9:]
+    width = dense.shape[2]
+    copies = []
+
+    def send(source, target):
+        copies.append(pltpu.make_async_copy(source, target, out_sems.at[len(copies)]))
+        copies[-1].start()
+
+    units = dense.shape[0] // 32
+    loads = [pltpu.make_async_copy(small_hbm, small, in_sems.at[0])]
+    for unit in range(units):
+        at = pl.ds(32 * unit, 32)
+        loads.append(
+            pltpu.make_async_copy(dense_hbm.at[at], dense.at[at], in_sems.at[len(loads)])
+        )
+    for source, target in zip(through, held):
+        loads.append(pltpu.make_async_copy(source, target, in_sems.at[len(loads)]))
+    for load in loads:
+        load.start()
+    loads[0].wait()
+    for number, (row, out) in enumerate(
+        (
+            (PROJECT, project_b),
+            (QUERY, query_b),
+            (VALUE, value_b),
+            (OUTPUT, output_b),
+            (FIRST_GAIN, first_gain),
+            (FIRST_SHIFT, first_shift),
+            (SHRINK, shrink_b),
+            (FINAL_GAIN, final_gain),
+            (FINAL_SHIFT, final_shift),
+        )
+    ):
+        vector[pl.ds(number * width, width)] = small[row]
+        send(vector.at[pl.ds(number * width, width)], out)
+    for piece in range(expand_b.shape[0] // width):
+        vector_wide[pl.ds(piece * width, width)] = small[EXPAND + piece]
+    send(vector_wide, expand_b)
+
+    def widen(unit):
+        loads[1 + unit].wait()
+        wide[unit] = dense[pl.ds(32 * unit, 32)].reshape(512, width).astype(f32)
+        return wide.at[unit]
+
+    for part in range(4):
+        send(widen(part), shrink.at[pl.ds(part * 512, 512)])
+        both = widen(4 + part)
+        send(both.at[pl.ds(0, width)], expand.at[:, pl.ds(part * 512, width)])
+        send(both.at[pl.ds(width, width)], expand.at[:, pl.ds(part * 512 + width, width)])
+    both = widen(8)
+    send(both.at[pl.ds(0, width)], query)
+    send(both.at[pl.ds(width, width)], key)
+    both = widen(9)
+    send(both.at[pl.ds(0, width)], value)
+    send(both.at[pl.ds(width, width)], output)
+    send(widen(10), project)
+    for load, source, target in zip(loads[1 + units :], held, through_out):
+        load.wait()
+        send(source, target)
+    for copy in copies:
+        copy.wait()
+
+
+def paired_body(
+    features,
+    quarter_turns,
+    heights,
+    widths,
+    frozen_scale,
+    frozen_shift,
+    first_kernel,
+    second_kernel,
+    project_weight,
+    project_bias,
+    query_weight,
+    query_bias,
+    key_weight,
+    value_weight,
+    value_bias,
+    output_weight,
+    output_bias,
+    first_gain,
+    first_shift,
+    expand_weight,
+    expand_bias,
+    shrink_weight,
+    shrink_bias,
+    final_gain,
+    final_shift,
+    cotangent,
+):
+    pages, rows, side, channels = features.shape
+    width = project_weight.shape[1]
+    hidden_units = expand_weight.shape[1]
+    length = rows * side
+    got = page_call(
+        side,
+        dict(
+            features=features.reshape(length, channels),
+            first_kernel=first_kernel.reshape(TAPS, channels, channels),
+            second_kernel=second_kernel.reshape(TAPS, channels, channels),
+            project_weight=project_weight,
+            query_weight=query_weight,
+            key_weight=key_weight,
+            value_weight=value_weight,
+            output_weight=output_weight,
+            expand_weight=expand_weight,
+            shrink_weight=shrink_weight,
+            cotangent=cotangent.reshape(length, width),
+            frozen_scale=frozen_scale,
+            frozen_shift=frozen_shift,
+            project_bias=project_bias,
+            query_bias=query_bias,
+            value_bias=value_bias,
+            output_bias=output_bias,
+            first_gain=first_gain,
+            first_shift=first_shift,
+            expand_bias=expand_bias,
+            shrink_bias=shrink_bias,
+            final_gain=final_gain,
+            final_shift=final_shift,
+            quarter_turns=quarter_turns,
+            heights=heights,
+            widths=widths,
+        ),
+    )
+    f32 = jnp.float32
+    square, vector = (width, width), (width,)
+    shapes = [
+        (channels, width),
+        vector,
+        square,
+        vector,
+        square,
+        square,
+        vector,
+        square,
+        vector,
+        vector,
+        vector,
+        (width, hidden_units),
+        (hidden_units,),
+        (hidden_units, width),
+        vector,
+        vector,
+        vector,
+    ]
+    hbm = pl.BlockSpec(memory_space=pl.ANY)
+    passed = (got.encoded, got.features_grad, got.first_grad, got.second_grad)
+    dense = got.dense_out
+    results = pl.pallas_call(
+        functools.partial(unpack_kernel, len(passed)),
+        out_shape=tuple(jax.ShapeDtypeStruct(value.shape, value.dtype) for value in passed)
+        + tuple(jax.ShapeDtypeStruct(shape, f32) for shape in shapes),
+        in_specs=[hbm] * (2 + len(passed)),
+        out_specs=tuple([hbm] * (len(passed) + len(shapes))),
+        scratch_shapes=[
+            pltpu.VMEM(dense.shape, jnp.bfloat16),
+            pltpu.VMEM((dense.shape[0] // 32, 512, width), f32),
+            pltpu.VMEM(got.small_out.shape, f32),
+            pltpu.VMEM((9 * width,), f32),
+            pltpu.VMEM((hidden_units,), f32),
+            pltpu.SemaphoreType.DMA((1 + dense.shape[0] // 32 + len(passed),)),
+            pltpu.SemaphoreType.DMA((32,)),
+        ]
+        + [pltpu.VMEM(value.shape, value.dtype) for value in passed],
+        compiler_params=pltpu.CompilerParams(vmem_limit_bytes=63 * 1024 * 1024),
+        name="unpack",
+    )(dense, got.small_out, *passed)
+    part_shape = (3, 3, channels // 16, channels // 2)
+    return (
+        results[0].reshape(pages, rows, side, width),
+        results[1].reshape(pages, rows, side, channels),
+        results[2].reshape(part_shape),
+        results[3].reshape(part_shape),
+    ) + tuple(results[len(passed) :])
+
+
 def solution(mesh):
+    paired = mesh.shape["strip"] == 2 and mesh.shape["page"] == 16
     return jax.shard_map(
-        body,
+        paired_body if paired else body,
         mesh=mesh,
         in_specs=(
             P("page", "strip", None, None),

time: 539 us -> 127 us (0.24); the launches traced: 531 us -> 127 us
  waiting for transfers between devices: 258 us -> 0 us
  Pallas kernels: 0 us -> 124 us
  matrix products: 116 us -> 0 us
  blocking collectives: 60.7 us -> 0 us
  local copies, waits for them, and re-layouts: 38 us -> 0 us
  other arithmetic: 22.4 us -> 0 us
  starting transfers between devices: 17.5 us -> 0 us
  between operations: 17.9 us -> 2.81 us
    psum x1 -> x0, waiting for transfers between devices: 129 us -> none  [body(): lax.psum((project_weight_grad, project_bias_grad, query_weight_grad, quer...]
    reduce_scatter x5 -> x0, waiting for transfers between devices: 125 us -> none  [the longest x1 71.7 us: body(): lax.psum_scatter(first_kernel_grad.astype(jnp.bfloat16), 'page', scatter_...]
    pallas_call x0 -> x2, Pallas kernels: none -> 124 us  [the longest x1 119 us: page_call(): pl.pallas_call(functools.partial(page_kernel, side, names), out_shape=tup...]
    dot_general x45 -> x0, matrix products: 92 us -> none  [the longest x18 26.5 us: kernel_grad(): jnp.einsum('prci,prco->io', window, upstream, preferred_element_type=jnp....]
    psum x1 -> x0, blocking collectives: 41.2 us -> none  [body(): lax.psum((project_weight_grad, project_bias_grad, query_weight_grad, quer...]
    unnamed x199 -> x0, local copies, waits for them, and re-layouts: 27.7 us -> none
    conv_general_dilated x4 -> x0, matrix products: 24.3 us -> none  [conv_valid(): lax.conv_general_dilated(padded, kernel, (1, 1), 'VALID', dimension_numbe...]
    all_gather x3 -> x0, blocking collectives: 19.5 us -> none  [the longest x1 7.35 us: body(): values_piece = lax.all_gather(values_local, 'strip', axis=1, tiled=True)]
  transfers between devices with their start and end apart: 14 -> 0, of which waited for: 6 -> 0; matrix products, arithmetic and copies ran while one was open for 11% -> 0% of each run, Pallas kernels for 0% -> 0%
where the time goes in v2:
time: 127 us
  Pallas kernels  124 us (98%)
  between operations  2.81 us (2%)
    pallas_call x1, Pallas kernels, page_call(): pl.pallas_call(functools.partial(page_kernel, side, names), out_shape=tup...  119 us
    pallas_call x1, Pallas kernels, paired_body(): pl.pallas_call(functools.partial(unpack_kernel, len(passed)), out_shape=t...  4.63 us

profile of v2, /device:TPU:0, one launch (start us, length us, event | category | flops | bytes accessed | tf_op | source)
XLA Modules:
  0.0 126.6 jit_solution(8954675400517770554)
XLA Ops:
  2.6 119.2 %page_step.1 = (bf16[512,256]{1,0:T(8,128)(2,1)}, f32[512,512]{1,0:T(8,128)}, f32[9,32,256]{2,1,0:T(8,128)}, f32[9,32,256]{2,1,0:T(8,128)}, bf16[352,16,256]{2,1,0:T(8,128)(2,1)}, /*index=5*/f32[24,256]{1,0:T(8,128)}) custom-call(bf16[512,512]{1,0:T(8,128)(2,1)} %bitcast.10, bf16[9,512,512]{2,1,0:T(8,128)(2,1)} %bitcast.8, bf16[9,512,512]{2,1,0:T(8,128)(2,1)} %bitcast.9, ...), custom_call_target="tpu_custom_call" | custom-call | tf_op jit(solution)/shard_map/page_step/pallas_call | solution.py:1352
  121.8 4.6 %unpack.1 = (bf16[512,256]{1,0:T(8,128)(2,1)}, f32[512,512]{1,0:T(8,128)}, f32[9,32,256]{2,1,0:T(8,128)}, f32[9,32,256]{2,1,0:T(8,128)}, f32[512,256]{1,0:T(8,12...) custom-call(bf16[352,16,256]{2,1,0:T(8,128)(2,1)} %get-tuple-element, ...), custom_call_target="tpu_custom_call" | custom-call | tf_op jit(solution)/shard_map/unpack/pallas_call | solution.py:1524

commit v3 on v2

--- a/solution.py
+++ b/solution.py
@@ -355,27 +355,32 @@
 CORE, X, Y, Z0, Z1 = range(5)
 STEPS = {CORE: 1, Y: 2, Z0: 4, Z1: 8}
 PLANE, COLUMN = (X, Y), (Z0, Z1)
+X_FIRST, X_LAST = ((CORE,), (X,), (Y,), COLUMN), ((CORE,), (Y,), COLUMN, (X,))
 DENSE = (
-    (64, ((CORE,), PLANE, COLUMN)),
-    (64, ((CORE,), PLANE, COLUMN)),
-    (64, ((CORE,), COLUMN, PLANE)),
-    (64, ((CORE,), PLANE, COLUMN)),
-    (64, ((CORE,), (X,), (Y,), COLUMN)),
-    (32, ((CORE,), (Y,), (X,), COLUMN)),
+    (64, X_LAST, 0.22, 0.21),
+    (64, X_FIRST, 0.56, 0.07),
+    (64, X_FIRST, 0.14, 0.44),
+    (64, X_LAST, 0.21, 0.08),
+    (64, X_LAST, 0.49, 0.95),
+    (32, X_LAST, 0.90, 0.45),
 )
 GRADS = (
-    ((Y,), (Z0,), (Z1,)),
-    ((Z0,), (Y,), (Z1,)),
-    ((Y,), (Z0,), (Z1,)),
-    ((Y,), (Z0,), (Z1,)),
-    ((Z0,), (Y,), (Z1,)),
-    ((Y,), (Z0,), (Z1,)),
+    (((Y,), COLUMN), 0.88),
+    (((Z0,), (Y,), (Z1,)), 0.66),
+    (((Y,), COLUMN), 0.23),
+    (((Y,), (Z0,), (Z1,)), 0.69),
+    (((Z0,), (Y,), (Z1,)), 0.56),
+    (((Y,), (Z0,), (Z1,)), 0.97),
 )
 ENDS, MIDDLE = 5, 6
 TAPS = 9
 LANES = 128
-WINDOW = 4.0
+WINDOW = 10.0
 DELAY = 2.0
+CHORE = 0.15
+T_DENSE, T_LATE, T_HALO, T_HIDDEN, T_SECOND, T_THIRD, T_FIRST = 31.0, 43.9, 46.0, 47.1, 53.0, 56.7, 60.7
+TICK = 0.55
+X_TRAFFIC = ((3.0, 10.5), (11.0, 5.0), (19.0, 10.5), (36.5, 6.5), (44.0, 12.5))
 PROJECT, QUERY, VALUE, OUTPUT, FIRST_GAIN, FIRST_SHIFT, SHRINK, FINAL_GAIN, FINAL_SHIFT, EXPAND = range(10)
 
 
@@ -471,10 +476,13 @@
         size = self.left[step + 1]
         offset = self.left[0] - self.left[step]
         total = self.current[pl.ds(slot_of(self.order[step], self.bits) * size, size)]
-        total = total.astype(jnp.float32)
-        for number in range(len(self.flights)):
-            total += self.parts[pl.ds(offset + number * size, size)].astype(jnp.float32)
-        total = total.astype(jnp.bfloat16)
+        if len(self.flights) == 1:
+            total = total + self.parts[pl.ds(offset, size)]
+        else:
+            total = total.astype(jnp.float32)
+            for number in range(len(self.flights)):
+                total += self.parts[pl.ds(offset + number * size, size)].astype(jnp.float32)
+            total = total.astype(jnp.bfloat16)
         if step == count - 1:
             self.keep(total)
             return
@@ -504,30 +512,54 @@
         self.sums[step + 1] = self.sums[step] + self.parts[step]
 
 
-def link_plan(units, window):
-    events = [(ready, 1, unit, 0) for unit, (ready, _) in enumerate(units)]
-    queue, busy, actions = [], {}, []
+def poll_times():
+    half = [1.3] + [0.42] * HEADS + [1.3]
+    times = [T_DENSE]
+    for spent in [0.5] + half + [0.4] + half:
+        times.append(times[-1] + spent)
+    for start, count in ((T_HALO, 1), (T_HIDDEN, 7), (T_SECOND, 7), (T_THIRD, 7), (T_FIRST, 7)):
+        times += [start + TICK * number for number in range(count)]
+    return sorted(times + [T_LATE])
+
+
+def link_plan(units):
+    polls = poll_times()
+
+    def poll(time):
+        return min([at for at in polls if at >= time], default=time)
+
+    events = [(poll(ready), 1, unit, 0) for unit, (ready, _, _) in enumerate(units)]
+    events += [(time, 0, -1, spent) for time, spent in X_TRAFFIC]
+    queue, busy, actions, free = [], {}, [], 0.0
     while events:
         events.sort()
         now, kind, unit, step = events.pop(0)
+        if unit < 0:
+            busy[X] = max(now, busy.get(X, 0.0)) + step
+            continue
+        if now >= polls[-1]:
+            now = max(now, free)
+            free = now + CHORE
         if kind == 0:
             actions.append((now, False, unit, step))
             step += 1
         if step < len(units[unit][1]):
-            left = sum(max(cost.values()) + DELAY for cost in units[unit][1][step:])
-            queue.append((-left, unit, step))
+            queue.append((units[unit][2][step], unit, step))
         queue.sort()
         held, waiting = set(), []
-        for left, unit, step in queue:
+        for rank, unit, step in queue:
             cost = units[unit][1][step]
-            if any(link in held or busy.get(link, 0.0) - now >= window for link in cost):
+            if any(
+                link in held or busy.get(link, 0.0) - now >= (0.01 if link == X else WINDOW)
+                for link in cost
+            ):
                 held.update(cost)
-                waiting.append((left, unit, step))
+                waiting.append((rank, unit, step))
                 continue
             for link, spent in cost.items():
                 busy[link] = max(now, busy.get(link, 0.0)) + spent
             actions.append((now, True, unit, step))
-            events.append((max(busy[link] for link in cost) + DELAY, 0, unit, step))
+            events.append((poll(max(busy[link] for link in cost) + DELAY), 0, unit, step))
         queue = waiting
     return actions
 
@@ -711,10 +743,9 @@
     pool, dense, owned = r.pool, r.dense, r.owned
     dense_units = len(DENSE)
     reducers, costs = [], []
-    ready_dense = [30.0, 30.2, 30.4, 30.6, 43.0, 44.0]
     unit_slots = 24
     begin, marks = 0, 0
-    for unit, (slots, order) in enumerate(DENSE):
+    for unit, (slots, order, rank, back_rank) in enumerate(DENSE):
         group = slots // 32
 
         def keep_dense(value, begin=begin, group=group, order=order):
@@ -729,14 +760,16 @@
                 dense.at[pl.ds(begin, slots)],
                 r.dense_parts.at[pl.ds(begin, slots)],
                 r.dense_sends.at[pl.ds(3 * unit, 3)],
-                r.dense_recvs.at[pl.ds(14 * unit, 14)],
+                r.dense_recvs.at[pl.ds(12 * unit, 12)],
                 True,
                 keep_dense,
             )
         )
-        costs.append((ready_dense[unit], link_costs(order, slots * 8192, True)))
+        ready = T_DENSE if unit < 4 else T_LATE if unit == 4 else T_HALO
+        ranks = [rank] * len(order) + [back_rank] * len(order)
+        costs.append((ready, link_costs(order, slots * 8192, True), ranks))
         begin += slots
-    for unit, order in enumerate(GRADS):
+    for unit, (order, rank) in enumerate(GRADS):
 
         def keep_grad(value, unit=unit):
             half = value.shape[1] // 2
@@ -753,14 +786,14 @@
                 peers,
                 pool.at[pl.ds(unit * unit_slots, unit_slots)],
                 r.parts.at[unit],
-                r.grad_sends.at[pl.ds(unit, 1)],
-                r.grad_recvs.at[pl.ds(3 * unit, 3)],
+                r.grad_sends.at[pl.ds(3 * unit, 3)],
+                r.grad_recvs.at[pl.ds(4 * unit, 4)],
                 False,
                 keep_grad,
             )
         )
-        made = 53.0 + unit if unit < 3 else 61.0 + unit - 3
-        costs.append((made, link_costs(order, 393216, False)))
+        made = (T_SECOND if unit < 3 else T_FIRST) + 2 * TICK * (unit % 3 + 1) - 0.01
+        costs.append((made, link_costs(order, 393216, False), [rank] * len(order)))
     small_order = (CORE, X, Y, Z0, Z1)
     small = r.small_sums
     reducers.append(
@@ -768,8 +801,9 @@
             small_order, peers, small, r.small_parts, r.small_sends, r.small_recvs
         )
     )
-    costs.append((44.0, [{CORE: 0.2}, {X: 0.5}, {Y: 0.5}, {ENDS: 0.5}, {MIDDLE: 1.0, ENDS: 0.5}]))
-    agenda = link_plan(costs, WINDOW)
+    small_costs = [{CORE: 0.2}, {X: 0.5}, {Y: 0.5}, {ENDS: 0.5}, {MIDDLE: 1.0, ENDS: 0.5}]
+    costs.append((T_HALO, small_costs, [0.0] * 5))
+    agenda = link_plan(costs)
 
     def work(spent):
         clock[0] += spent
@@ -813,6 +847,8 @@
                 window = pl.ds(start + side * down, count)
                 term = dot(x3[2 - across, window], weight[tap])
             total = term if total is None else total + term
+            if transposed and across == 2:
+                work(TICK)
         return total
 
     x3 = r.x3
@@ -945,20 +981,25 @@
     keys_of(1)
     attend(1)
 
-    shares_t = r.shares_t
     for head in range(HEADS):
-        channel = pl.ds(head * head_size, head_size)
         first_peak, first_sum = stat[head, 0:1], stat[head, 1:2]
         second_peak, second_sum = stat[head, 2:3], stat[head, 3:4]
         peak = jnp.maximum(first_peak, second_peak)
         first_scale, second_scale = jnp.exp(first_peak - peak), jnp.exp(second_peak - peak)
         total = first_scale * first_sum + second_scale * second_sum
-        first_scale, second_scale = first_scale / total, second_scale / total
-        stat[head, 4:5] = first_scale
-        stat[head, 5:6] = second_scale
-        shares_t[0, channel] = jnp.broadcast_to(first_scale, (head_size, length))
-        shares_t[1, channel] = jnp.broadcast_to(second_scale, (head_size, length))
-    mixed = (shares_t[0] * mixed_parts[0] + shares_t[1] * mixed_parts[1]).T
+        stat[head, 4:5] = first_scale / total
+        stat[head, 5:6] = second_scale / total
+
+    def shares_t(which):
+        return jnp.concatenate(
+            [
+                jnp.broadcast_to(stat[head, 4 + which : 5 + which], (head_size, length))
+                for head in range(HEADS)
+            ],
+            axis=0,
+        )
+
+    mixed = (shares_t(0) * mixed_parts[0] + shares_t(1) * mixed_parts[1]).T
     combined = r.combined
     combined[...] = low(mixed)
 
@@ -1032,13 +1073,13 @@
     for part in range(pieces // 2):
         both = dot(ff_t, d_expanded[:, pl.ds(part * 512, 512)])
         put(4 + part, jnp.concatenate([both[:, :width], both[:, width:]], axis=0))
-    settle(30.0)
+    settle(T_DENSE)
 
     deltas = r.deltas
     d_scaled = r.d_scaled
     total = None
     for which in range(2):
-        scaled = low(d_combined[...].astype(f32) * shares_t[which].T)
+        scaled = low(d_combined[...].astype(f32) * shares_t(which).T)
         d_scaled[which] = scaled
         term = scaled.T.astype(f32) * mixed_parts[which]
         total = term if total is None else total + term
@@ -1073,7 +1114,7 @@
         for head in range(HEADS):
             spare_scaled[:, pl.ds(head * width, width)] = only(head, d_scaled[which])
         d_values = low(dot(stacked(which), heads_down(spare_scaled)))
-        work(1.2)
+        work(1.3)
         for head in range(HEADS):
             d_prob = dot_nt(values[at], spare_scaled[:, pl.ds(head * width, width)])
             d_prob = d_prob - deltas[head, which : which + 1]
@@ -1087,9 +1128,9 @@
             d_queries_t[channel] += dot(
                 keys_t[which, channel], jnp.concatenate(pieces_here, axis=1)
             )
-            work(0.3)
+            work(0.42)
         d_keys = low(dot(stacked(which), heads_down(spare_query)) * factor)
-        work(1.2)
+        work(1.3)
         d_rows = dot_nt(d_keys, r.w_key[...]) + dot_nt(d_values, r.w_value[...])
         small[0, VALUE : VALUE + 1] += row_sum(d_values)
         return (
@@ -1101,7 +1142,7 @@
     d_other, key_grad, value_grad = attend_back(1)
     d_combined[...] = low(d_other)
     d_rows_copy = exchange(d_combined, r.d_rows_in, peers[(X,)])
-    work(0.3)
+    work(0.4)
     d_own, more_key, more_value = attend_back(0)
     d_queries = low(d_queries_t[...].T * factor)
     small[0, QUERY : QUERY + 1] = row_sum(d_queries)
@@ -1114,7 +1155,7 @@
         9,
         jnp.concatenate([value_grad + more_value, dot(combined[...].T, d_attended[...])], axis=0),
     )
-    settle(43.0)
+    settle(T_LATE)
     d_source = d_first[...] + dot_nt(d_queries, r.w_query[...]) + d_own
     d_rows_copy.wait()
     d_source = low(d_source + r.d_rows_in[...].astype(f32))
@@ -1157,7 +1198,7 @@
     late_ext[aligned(strip * (length + edge), edge)] = blank
     spread(late_ext, x3, 2, rows)
     put(10, dot(block[...].T, d_source))
-    settle(44.0)
+    settle(T_HALO)
     for copy in hidden_copies:
         copy.wait()
     hidden_relay = share(r.hidden_all, other_lanes, 0, 1, peers[(CORE,)])
@@ -1165,11 +1206,11 @@
     spread(late_ext, x3, 0, 2)
     spread(late_ext, x3, rows + 2, 2)
     early = hidden
+    settle(T_HIDDEN)
     for part in range(2):
         at = pl.ds(part * half_rows, half_rows)
         d_hidden = conv(x3, r.w_second, part * half_rows, half_rows, True)
         early[at] = low(d_hidden * r.slope_first[at])
-        work(1.5)
     early_copies = spread_out(early, side, r.early_page)
     page3 = r.page3
 
@@ -1194,6 +1235,8 @@
                 right = jnp.concatenate([page3[page, across, window] for across in range(3)], axis=1)
                 term = dot(left[page], right)
                 product = term if product is None else product + term
+                if page == 0:
+                    work(TICK)
             product = low(product)
             unit = first_unit + down
             order = reducers[dense_units + unit].order
@@ -1204,23 +1247,23 @@
                     pool[unit * unit_slots + slot_of(flat(order), place) * 3 + across] = product[
                         chip * size : (chip + 1) * size, across * LANES : (across + 1) * LANES
                     ]
-            work(1.0)
+            work(TICK)
 
     for copy in late_copies + [hidden_relay, feat_relay]:
         copy.wait()
     spread_pages(r.late_page)
-    settle(52.0)
+    settle(T_SECOND)
     kernel_grads(r.hidden_all, 0)
     spread(early, x3, 0, rows + 2)
+    settle(T_THIRD)
     for part in range(2):
         at = pl.ds(part * half, half)
         direct[at] = conv(x3, r.w_first, part * half, half, True) + direct[at]
-        work(1.3)
     store(direct, r.features_grad)
     for copy in early_copies:
         copy.wait()
     spread_pages(r.early_page)
-    settle(60.0)
+    settle(T_FIRST)
     kernel_grads(r.features_all, 3)
     settle(1e9)
     store(small.at[5], r.small_out)
@@ -1234,8 +1277,8 @@
         finals.append((copy, which, here, out))
     for copy, which, here, out in finals:
         copy.wait()
-        here[:, :, aligned(core * LANES, LANES, LANES)] = owned[which, core].astype(f32)
-        here[:, :, aligned((1 - core) * LANES, LANES, LANES)] = r.owned_sib[which].astype(f32)
+        here[:, :, aligned(core * LANES, LANES, LANES)] = owned[which, core]
+        here[:, :, aligned((1 - core) * LANES, LANES, LANES)] = r.owned_sib[which]
         store(here, out)
     for copy in stores:
         copy.wait()
@@ -1257,8 +1300,8 @@
     outs = dict(
         encoded=((length, width), bf16),
         features_grad=((length, channels), f32),
-        first_grad=((TAPS, channels // 16, channels // 2), f32),
-        second_grad=((TAPS, channels // 16, channels // 2), f32),
+        first_grad=((TAPS, channels // 16, channels // 2), bf16),
+        second_grad=((TAPS, channels // 16, channels // 2), bf16),
         dense_out=(dense_shape, bf16),
         small_out=((24, width), f32),
     )
@@ -1287,8 +1330,8 @@
         v_final_shift=((width,), f32),
         encoded_here=((length, width), bf16),
         direct=((length, channels), f32),
-        first_here=((TAPS, channels // 16, channels // 2), f32),
-        second_here=((TAPS, channels // 16, channels // 2), f32),
+        first_here=((TAPS, channels // 16, channels // 2), bf16),
+        second_here=((TAPS, channels // 16, channels // 2), bf16),
         table_row=((side, width), f32),
         table_col=((side, width), f32),
         bias_row=((side, LANES), f32),
@@ -1312,7 +1355,6 @@
         stat=((HEADS, 8, length), f32),
         deltas=((HEADS, 8, length), f32),
         mixed_parts=((2, width, length), f32),
-        shares_t=((2, width, length), f32),
         combined=((length, width), bf16),
         activated=((length, hidden_units), bf16),
         d_expanded=((length, hidden_units), bf16),
@@ -1341,10 +1383,10 @@
         out_sems=(6,),
         pair_sends=(20,),
         pair_recvs=(20,),
-        grad_sends=(6,),
-        grad_recvs=(18,),
+        grad_sends=(3 * len(GRADS),),
+        grad_recvs=(4 * len(GRADS),),
         dense_sends=(3 * len(DENSE),),
-        dense_recvs=(14 * len(DENSE),),
+        dense_recvs=(12 * len(DENSE),),
         small_sends=(5,),
         small_recvs=(5,),
     )
@@ -1369,7 +1411,10 @@
     through, refs = refs[:passed], refs[passed:]
     through_out, refs = refs[:passed], refs[passed:]
     held, refs = refs[len(refs) - passed :], refs[: len(refs) - passed]
-    outs, (dense, wide, small, vector, vector_wide, in_sems, out_sems) = refs[:-7], refs[-7:]
+    outs, (dense, wide, small, vector, vector_wide, wide_grads, in_sems, out_sems) = (
+        refs[:-8],
+        refs[-8:],
+    )
     project, project_b, query, query_b, key, value, value_b, output, output_b = outs[:9]
     first_gain, first_shift, expand, expand_b, shrink, shrink_b, final_gain, final_shift = outs[9:]
     width = dense.shape[2]
@@ -1427,8 +1472,11 @@
     send(both.at[pl.ds(0, width)], value)
     send(both.at[pl.ds(width, width)], output)
     send(widen(10), project)
-    for load, source, target in zip(loads[1 + units :], held, through_out):
+    for number, (load, source, target) in enumerate(zip(loads[1 + units :], held, through_out)):
         load.wait()
+        if source.dtype != target.dtype:
+            wide_grads[number % 2] = source[...].astype(f32)
+            source = wide_grads.at[number % 2]
         send(source, target)
     for copy in copies:
         copy.wait()
@@ -1523,7 +1571,8 @@
     dense = got.dense_out
     results = pl.pallas_call(
         functools.partial(unpack_kernel, len(passed)),
-        out_shape=tuple(jax.ShapeDtypeStruct(value.shape, value.dtype) for value in passed)
+        out_shape=tuple(jax.ShapeDtypeStruct(value.shape, f32 if value.ndim == 3 else value.dtype)
+            for value in passed)
         + tuple(jax.ShapeDtypeStruct(shape, f32) for shape in shapes),
         in_specs=[hbm] * (2 + len(passed)),
         out_specs=tuple([hbm] * (len(passed) + len(shapes))),
@@ -1533,6 +1582,7 @@
             pltpu.VMEM(got.small_out.shape, f32),
             pltpu.VMEM((9 * width,), f32),
             pltpu.VMEM((hidden_units,), f32),
+            pltpu.VMEM((2,) + got.first_grad.shape, f32),
             pltpu.SemaphoreType.DMA((1 + dense.shape[0] // 32 + len(passed),)),
             pltpu.SemaphoreType.DMA((32,)),
         ]

time: 127 us -> 120 us (0.945)
  Pallas kernels: 124 us -> 117 us
    pallas_call x1, Pallas kernels: 119 us -> 113 us  [page_call(): pl.pallas_call(functools.partial(page_kernel, side, names), out_shape=tup...]
where the time goes in v3:
time: 120 us
  Pallas kernels  117 us (98%)
  between operations  2.81 us (2%)
    pallas_call x1, Pallas kernels, page_call(): pl.pallas_call(functools.partial(page_kernel, side, names), out_shape=tup...  113 us
    pallas_call x1, Pallas kernels, paired_body(): pl.pallas_call(functools.partial(unpack_kernel, len(passed)), out_shape=t...  4.63 us

profile of v3, /device:TPU:0, one launch (start us, length us, event | category | flops | bytes accessed | tf_op | source)
XLA Modules:
  0.0 120.2 jit_solution(8389764009374511704)
XLA Ops:
  2.6 112.8 %page_step.1 = (bf16[512,256]{1,0:T(8,128)(2,1)}, f32[512,512]{1,0:T(8,128)}, bf16[9,32,256]{2,1,0:T(8,128)(2,1)}, bf16[9,32,256]{2,1,0:T(8,128)(2,1)}, bf16[352...) custom-call(bf16[512,512]{1,0:T(8,128)(2,1)} %bitcast.10, bf16[9,512,512]{2,1,0:T(8,128)(2,1)} %bitcast.8, ...), custom_call_target="tpu_custom_call" | custom-call | tf_op jit(solution)/shard_map/page_step/pallas_call | solution.py:1394
  115.4 4.6 %unpack.1 = (bf16[512,256]{1,0:T(8,128)(2,1)}, f32[512,512]{1,0:T(8,128)}, f32[9,32,256]{2,1,0:T(8,128)}, f32[9,32,256]{2,1,0:T(8,128)}, f32[512,256]{1,0:T(8,12...) custom-call(bf16[352,16,256]{2,1,0:T(8,128)(2,1)} %get-tuple-element, ...), custom_call_target="tpu_custom_call" | custom-call | tf_op jit(solution)/shard_map/unpack/pallas_call | solution.py:1572

commit v4 on v3

--- a/solution.py
+++ b/solution.py
@@ -813,6 +813,10 @@
                 reducers[unit].begin(step)
             else:
                 reducers[unit].end(step)
+                if unit < dense_units and step + 1 == len(costs[unit][1]):
+                    first = sum(slots for slots, _, _, _ in DENSE[:unit])
+                    at = pl.ds(first, DENSE[unit][0])
+                    store(dense.at[at], r.dense_out.at[at])
 
     stores = []
 
@@ -1267,7 +1271,6 @@
     kernel_grads(r.features_all, 3)
     settle(1e9)
     store(small.at[5], r.small_out)
-    store(dense, r.dense_out)
     finals = []
     for which, here, out in (
         (1, r.first_here, r.first_grad),
@@ -1380,7 +1383,7 @@
     )
     sem_shapes = dict(
         load_sems=(23,),
-        out_sems=(6,),
+        out_sems=(5 + len(DENSE),),
         pair_sends=(20,),
         pair_recvs=(20,),
         grad_sends=(3 * len(GRADS),),
@@ -1465,6 +1468,12 @@
         both = widen(4 + part)
         send(both.at[pl.ds(0, width)], expand.at[:, pl.ds(part * 512, width)])
         send(both.at[pl.ds(width, width)], expand.at[:, pl.ds(part * 512 + width, width)])
+    for number, (load, source, target) in enumerate(zip(loads[1 + units :], held, through_out)):
+        load.wait()
+        if source.dtype != target.dtype:
+            wide_grads[number % 2] = source[...].astype(f32)
+            source = wide_grads.at[number % 2]
+        send(source, target)
     both = widen(8)
     send(both.at[pl.ds(0, width)], query)
     send(both.at[pl.ds(width, width)], key)
@@ -1472,12 +1481,6 @@
     send(both.at[pl.ds(0, width)], value)
     send(both.at[pl.ds(width, width)], output)
     send(widen(10), project)
-    for number, (load, source, target) in enumerate(zip(loads[1 + units :], held, through_out)):
-        load.wait()
-        if source.dtype != target.dtype:
-            wide_grads[number % 2] = source[...].astype(f32)
-            source = wide_grads.at[number % 2]
-        send(source, target)
     for copy in copies:
         copy.wait()
 

time: 120 us -> 121 us (level)
  no operation moved by 1% of the time
where the time goes in v4:
time: 121 us; the launch traced here: 120 us
  Pallas kernels  118 us (98%)
  between operations  2.81 us (2%)
    pallas_call x1, Pallas kernels, page_call(): pl.pallas_call(functools.partial(page_kernel, side, names), out_shape=tup...  113 us
    pallas_call x1, Pallas kernels, paired_body(): pl.pallas_call(functools.partial(unpack_kernel, len(passed)), out_shape=t...  4.79 us

profile of v4, /device:TPU:0, one launch (start us, length us, event | category | flops | bytes accessed | tf_op | source)
XLA Modules:
  0.0 120.4 jit_solution(1526874016988573374)
XLA Ops:
  2.6 112.8 %page_step.1 = (bf16[512,256]{1,0:T(8,128)(2,1)}, f32[512,512]{1,0:T(8,128)}, bf16[9,32,256]{2,1,0:T(8,128)(2,1)}, bf16[9,32,256]{2,1,0:T(8,128)(2,1)}, bf16[352...) custom-call(bf16[512,512]{1,0:T(8,128)(2,1)} %bitcast.10, bf16[9,512,512]{2,1,0:T(8,128)(2,1)} %bitcast.8, ...), custom_call_target="tpu_custom_call" | custom-call | tf_op jit(solution)/shard_map/page_step/pallas_call | solution.py:1397
  115.4 4.8 %unpack.1 = (bf16[512,256]{1,0:T(8,128)(2,1)}, f32[512,512]{1,0:T(8,128)}, f32[9,32,256]{2,1,0:T(8,128)}, f32[9,32,256]{2,1,0:T(8,128)}, f32[512,256]{1,0:T(8,12...) custom-call(bf16[352,16,256]{2,1,0:T(8,128)(2,1)} %get-tuple-element, ...), custom_call_target="tpu_custom_call" | custom-call | tf_op jit(solution)/shard_map/unpack/pallas_call | solution.py:1575
